TPU v7x, 128 devices: a whole 4x4x4 slice. The times are simulated.
128 devices in a mesh: ch: 4 (over y), rows: 32 (over x, z, core).
Axes of the slice: x: 4, y: 4, z: 4, core: 2. Of those that a mesh axis runs over, the one named last changes fastest.
Arguments:
- features: bfloat16 [2, 32, 512, 512], P(None, 'rows', None, 'ch'), may hold values from -6 to 6
- lengths: int32 [2, 32], P(None, 'rows'), may hold values from 128 to 512, as said below
- input_gain: bfloat16 [512], P(('ch', 'rows')), may hold values from 0.5 to 1.5
- input_bias: bfloat16 [512], P(('ch', 'rows')), may hold values from -1.25 to 1.25
- proj_weight: bfloat16 [512, 768], P(('ch', 'rows')), may hold values from -0.25 to 0.25
- proj_bias: bfloat16 [768], P(('ch', 'rows')), may hold values from -1.25 to 1.25
- conv_weight: bfloat16 [768, 48, 128], P(('ch', 'rows')), may hold values from -0.078125 to 0.078125
- conv_bias: bfloat16 [768], P(('ch', 'rows')), may hold values from -1.25 to 1.25
- encoder_gain: bfloat16 [768], P(('ch', 'rows')), may hold values from 0.5 to 1.5
- encoder_bias: bfloat16 [768], P(('ch', 'rows')), may hold values from -1.25 to 1.25
- attend_weight: bfloat16 [768, 2304], P(('ch', 'rows')), may hold values from -0.3125 to 0.3125
- query_bias: bfloat16 [768], P(('ch', 'rows')), may hold values from -1.25 to 1.25
- value_bias: bfloat16 [768], P(('ch', 'rows')), may hold values from -1.25 to 1.25
- output_weight: bfloat16 [768, 768], P(('ch', 'rows')), may hold values from -1.75 to 1.75
- output_bias: bfloat16 [768], P(('ch', 'rows')), may hold values from -3.5 to 3.5
- attend_gain: bfloat16 [768], P(('ch', 'rows')), may hold values from 0.5 to 1.5
- attend_bias: bfloat16 [768], P(('ch', 'rows')), may hold values from -1.25 to 1.25
- hidden_weight: bfloat16 [768, 3072], P(('ch', 'rows')), may hold values from -0.21875 to 0.21875
- hidden_bias: bfloat16 [3072], P(('ch', 'rows')), may hold values from -1.25 to 1.25
- return_weight: bfloat16 [3072, 768], P(('ch', 'rows')), may hold values from -0.109375 to 0.109375
- return_bias: bfloat16 [768], P(('ch', 'rows')), may hold values from -1.25 to 1.25
- final_gain: bfloat16 [768], P(('ch', 'rows')), may hold values from 0.5 to 1.5
- final_bias: bfloat16 [768], P(('ch', 'rows')), may hold values from -1.25 to 1.25
- out_grad: bfloat16 [2, 32, 512, 768], P(None, 'rows', 'ch'), may hold values from -6 to 6
Outputs:
- output: bfloat16 [2, 32, 512, 768], P(None, 'rows', 'ch')
- features_grad: float32 [2, 32, 512, 512], P(None, 'rows', None, 'ch')
- input_gain_grad: float32 [512], P(('ch', 'rows'))
- input_bias_grad: float32 [512], P(('ch', 'rows'))
- proj_weight_grad: float32 [512, 768], P(('ch', 'rows'))
- proj_bias_grad: float32 [768], P(('ch', 'rows'))
- conv_weight_grad: float32 [768, 48, 128], P(('ch', 'rows'))
- conv_bias_grad: float32 [768], P(('ch', 'rows'))
- encoder_gain_grad: float32 [768], P(('ch', 'rows'))
- encoder_bias_grad: float32 [768], P(('ch', 'rows'))
- attend_weight_grad: float32 [768, 2304], P(('ch', 'rows'))
- query_bias_grad: float32 [768], P(('ch', 'rows'))
- value_bias_grad: float32 [768], P(('ch', 'rows'))
- output_weight_grad: float32 [768, 768], P(('ch', 'rows'))
- output_bias_grad: float32 [768], P(('ch', 'rows'))
- attend_gain_grad: float32 [768], P(('ch', 'rows'))
- attend_bias_grad: float32 [768], P(('ch', 'rows'))
- hidden_weight_grad: float32 [768, 3072], P(('ch', 'rows'))
- hidden_bias_grad: float32 [3072], P(('ch', 'rows'))
- return_weight_grad: float32 [3072, 768], P(('ch', 'rows'))
- return_bias_grad: float32 [768], P(('ch', 'rows'))
- final_gain_grad: float32 [768], P(('ch', 'rows'))
- final_bias_grad: float32 [768], P(('ch', 'rows'))
Inputs may be any that keep to these rules, and one draw needn't show every extreme that they name: `lengths`: each entry is the number of valid frames at the start of one utterance slot of 512 frames; in every column one of the 2 entries exceeds 3 * 128.
All inputs are finite; a program needn't handle non-finite values.
Results may differ from a plain program's by a relative error of at most 0.033.
Values may be sent and summed in bfloat16 or wider, within the bound.
A program may use at most 192 MiB of HBM per device.

v0:
```python
import jax
import jax.numpy as jnp
from jax import lax
from jax.sharding import PartitionSpec as P

HEAD_DIM = 64


EPS = 1e-05
NEGATIVE = -1000000000.0
TAP_STEP = 8


def widen(values):
    return values.astype(jnp.float32)


def smooth(values):
    return jax.nn.gelu(values, approximate=False)


def row_sums(first, second):
    return lax.psum((first, second), "ch")


def sum_parts(terms):
    return lax.psum_scatter(terms, "ch", scatter_dimension=2, tiled=True)


def gather_full(slopes):
    return lax.all_gather(slopes, "ch", axis=2, tiled=True)


def norm_split(values, gain, shift):
    total = values.shape[-1] * lax.axis_size("ch")
    first, second = row_sums(
        jnp.sum(values, axis=-1, keepdims=True), jnp.sum(values * values, axis=-1, keepdims=True)
    )
    mean = first / total
    spread = second / total - mean * mean
    scale = lax.rsqrt(spread + EPS)
    normal = (values - mean) * scale
    return (normal * gain + shift, normal, scale)


def norm_split_back(incoming, normal, scale, gain):
    total = incoming.shape[-1] * lax.axis_size("ch")
    scaled = incoming * gain
    first, second = row_sums(
        jnp.sum(scaled, axis=-1, keepdims=True), jnp.sum(scaled * normal, axis=-1, keepdims=True)
    )
    result = scale * (scaled - first / total - normal * (second / total))
    return (result, jnp.sum(incoming * normal, axis=0), jnp.sum(incoming, axis=0))


def project(left, weight, pieces):
    rows = left.shape[0]
    terms = jnp.dot(left, weight, preferred_element_type=jnp.float32)
    return sum_parts(terms.reshape(rows, pieces, weight.shape[1] // pieces))


def spread_full(slopes):
    rows = slopes.shape[0]
    return gather_full(slopes.reshape(rows, 1, slopes.shape[1]))[:, 0]


def tap_rows(source, starts, rows):
    return jnp.stack([lax.dynamic_slice_in_dim(source, begin, rows, 0) for begin in starts], axis=1)


def conv_apply(padded, kernel, rows):
    width, inner, taps = kernel.shape
    groups = width // inner

    def step(index, total):
        first = index * TAP_STEP
        slab = tap_rows(padded, [first + offset for offset in range(TAP_STEP)], rows)
        slab = slab.reshape(rows, TAP_STEP, groups, inner)
        block = lax.dynamic_slice_in_dim(kernel, first, TAP_STEP, 2).reshape(
            groups, inner, inner, TAP_STEP
        )
        part = jnp.einsum("tkgi,goik->tgo", slab, block, preferred_element_type=jnp.float32)
        return total + part.reshape(rows, width)

    return lax.fori_loop(0, taps // TAP_STEP, step, jnp.zeros((rows, width), jnp.float32))


def conv_grads(padded, slope_padded, kernel, slope, rows):
    width, inner, taps = kernel.shape
    groups = width // inner
    slope_groups = slope.reshape(rows, groups, inner)

    def step(index, carry):
        weight_total, input_total = carry
        first = index * TAP_STEP
        slab = tap_rows(padded, [first + offset for offset in range(TAP_STEP)], rows)
        slab = slab.reshape(rows, TAP_STEP, groups, inner)
        block = lax.dynamic_slice_in_dim(kernel, first, TAP_STEP, 2).reshape(
            groups, inner, inner, TAP_STEP
        )
        part = jnp.einsum("tkgi,tgo->goik", slab, slope_groups, preferred_element_type=jnp.float32)
        weight_total = lax.dynamic_update_slice_in_dim(
            weight_total, part.reshape(width, inner, TAP_STEP), first, 2
        )
        mirror = tap_rows(slope_padded, [taps - first - offset for offset in range(TAP_STEP)], rows)
        mirror = mirror.reshape(rows, TAP_STEP, groups, inner)
        spread_back = jnp.einsum(
            "tkgo,goik->tgi", mirror, block, preferred_element_type=jnp.float32
        )
        return (weight_total, input_total + spread_back.reshape(rows, width))

    start = (jnp.zeros((width, inner, taps), jnp.float32), jnp.zeros((rows, width), jnp.float32))
    return lax.fori_loop(0, taps // TAP_STEP, step, start)


def masked_scores(query, keys, live, scale):
    raw = jnp.einsum("thd,shd->hts", query, keys, preferred_element_type=jnp.float32) * scale
    return jnp.where(live[None, None, :], raw, NEGATIVE)


def run_micro(frames, upstream, params, length):
    (
        input_gain,
        input_bias,
        proj_weight,
        proj_bias,
        conv_weight,
        conv_bias,
        encoder_gain,
        encoder_bias,
        attend_weight,
        query_bias,
        value_bias,
        output_weight,
        output_bias,
        attend_gain,
        attend_bias,
        hidden_weight,
        hidden_bias,
        return_weight,
        return_bias,
        final_gain,
        final_bias,
    ) = params
    lowtype = jnp.bfloat16
    rows = frames.shape[0]
    part_width = conv_weight.shape[0]
    heads = part_width // HEAD_DIM
    taps = conv_weight.shape[2]
    scale = HEAD_DIM ** (-0.5)
    live = jnp.arange(rows, dtype=jnp.int32) < length
    keep = live.astype(jnp.float32)
    source = widen(frames)
    normed_in, normal_in, scale_in = norm_split(source, widen(input_gain), widen(input_bias))
    normed_low = normed_in.astype(lowtype)
    projected = (project(normed_low, proj_weight, 1)[:, 0] + widen(proj_bias)) * keep[:, None]
    proj_low = projected.astype(lowtype)
    padded = jnp.pad(proj_low, ((taps // 2, taps // 2), (0, 0)))
    before = conv_apply(padded, conv_weight, rows) + widen(conv_bias)
    summed_pos = projected + smooth(before)
    encoded, normal_enc, scale_enc = norm_split(
        summed_pos, widen(encoder_gain), widen(encoder_bias)
    )
    encoded_low = encoded.astype(lowtype)
    joint = project(encoded_low, attend_weight, 3)
    query = (joint[:, 0] + widen(query_bias)).astype(lowtype).reshape(rows, heads, HEAD_DIM)
    key_rows = joint[:, 1].astype(lowtype).reshape(rows, heads, HEAD_DIM)
    value_rows = (joint[:, 2] + widen(value_bias)).astype(lowtype).reshape(rows, heads, HEAD_DIM)
    scores = masked_scores(query, key_rows, live, scale)
    top = jnp.max(scores, axis=-1, keepdims=True)
    expo = jnp.exp(scores - top)
    denom = jnp.sum(expo, axis=-1, keepdims=True)
    probs = expo / denom
    logsum = top + jnp.log(denom)
    context = jnp.einsum(
        "hts,shd->thd", probs.astype(lowtype), value_rows, preferred_element_type=jnp.float32
    )
    context_low = context.reshape(rows, part_width).astype(lowtype)
    attended = project(context_low, output_weight, 1)[:, 0] + widen(output_bias)
    attn_sum = encoded + attended
    attn_norm, normal_att, scale_att = norm_split(attn_sum, widen(attend_gain), widen(attend_bias))
    attn_low = attn_norm.astype(lowtype)
    pre_hidden = project(attn_low, hidden_weight, 1)[:, 0] + widen(hidden_bias)
    activated = smooth(pre_hidden).astype(lowtype)
    outer = project(activated, return_weight, 1)[:, 0] + widen(return_bias)
    ffn_sum = attn_norm + outer
    result, normal_fin, scale_fin = norm_split(ffn_sum, widen(final_gain), widen(final_bias))
    grad_ffn, final_gain_grad, final_bias_grad = norm_split_back(
        widen(upstream), normal_fin, scale_fin, widen(final_gain)
    )
    slope_outer = grad_ffn.astype(lowtype)
    return_bias_grad = jnp.sum(widen(slope_outer), axis=0)
    outer_full = spread_full(slope_outer)
    return_weight_grad = jnp.einsum(
        "tf,td->fd", activated, outer_full, preferred_element_type=jnp.float32
    )
    grad_act = jnp.einsum(
        "td,fd->tf", outer_full, return_weight, preferred_element_type=jnp.float32
    )
    unused, pullback = jax.vjp(smooth, pre_hidden)
    slope_inner = pullback(grad_act)[0].astype(lowtype)
    hidden_bias_grad = jnp.sum(widen(slope_inner), axis=0)
    inner_full = spread_full(slope_inner)
    hidden_weight_grad = jnp.einsum(
        "tc,tf->cf", attn_low, inner_full, preferred_element_type=jnp.float32
    )
    grad_norm2 = grad_ffn + jnp.einsum(
        "tf,cf->tc", inner_full, hidden_weight, preferred_element_type=jnp.float32
    )
    grad_attn, attend_gain_grad, attend_bias_grad = norm_split_back(
        grad_norm2, normal_att, scale_att, widen(attend_gain)
    )
    slope_att = grad_attn.astype(lowtype)
    output_bias_grad = jnp.sum(widen(slope_att), axis=0)
    att_full = spread_full(slope_att)
    output_weight_grad = jnp.einsum(
        "tc,td->cd", context_low, att_full, preferred_element_type=jnp.float32
    )
    grad_context = jnp.einsum(
        "td,cd->tc", att_full, output_weight, preferred_element_type=jnp.float32
    )
    grad_context = grad_context.astype(lowtype).reshape(rows, heads, HEAD_DIM)
    again = masked_scores(query, key_rows, live, scale)
    weights_back = jnp.exp(again - logsum)
    weights_low = weights_back.astype(lowtype)
    grad_probs = jnp.einsum(
        "thd,shd->hts", grad_context, value_rows, preferred_element_type=jnp.float32
    )
    value_part = jnp.einsum(
        "hts,thd->shd", weights_low, grad_context, preferred_element_type=jnp.float32
    )
    centre = jnp.sum(weights_back * grad_probs, axis=-1, keepdims=True)
    slope_scores = (weights_back * (grad_probs - centre)).astype(lowtype)
    grad_query = (
        jnp.einsum("hts,shd->thd", slope_scores, key_rows, preferred_element_type=jnp.float32)
        * scale
    )
    grad_query = grad_query.reshape(rows, part_width).astype(lowtype)
    key_part = (
        jnp.einsum("hts,thd->shd", slope_scores, query, preferred_element_type=jnp.float32) * scale
    )
    grad_key = key_part.reshape(rows, part_width).astype(lowtype)
    grad_value = value_part.reshape(rows, part_width).astype(lowtype)
    slope_joint = jnp.stack([grad_query, grad_key, grad_value], axis=1)
    query_bias_grad = jnp.sum(widen(grad_query), axis=0)
    value_bias_grad = jnp.sum(widen(grad_value), axis=0)
    joint_full = gather_full(slope_joint).reshape(rows, attend_weight.shape[1])
    attend_weight_grad = jnp.einsum(
        "tc,tk->ck", encoded_low, joint_full, preferred_element_type=jnp.float32
    )
    grad_encoded = grad_attn + jnp.einsum(
        "tk,ck->tc", joint_full, attend_weight, preferred_element_type=jnp.float32
    )
    grad_pos, encoder_gain_grad, encoder_bias_grad = norm_split_back(
        grad_encoded, normal_enc, scale_enc, widen(encoder_gain)
    )
    unused, pullback = jax.vjp(smooth, before)
    slope_conv = pullback(grad_pos)[0].astype(lowtype)
    conv_bias_grad = jnp.sum(widen(slope_conv), axis=0)
    slope_padded = jnp.pad(slope_conv, ((taps // 2, taps // 2), (0, 0)))
    conv_weight_grad, grad_conv_in = conv_grads(padded, slope_padded, conv_weight, slope_conv, rows)
    rounded = (grad_pos + grad_conv_in).astype(lowtype)
    slope_proj = jnp.where(live[:, None], rounded, jnp.zeros_like(rounded))
    proj_bias_grad = jnp.sum(widen(slope_proj), axis=0)
    proj_full = spread_full(slope_proj)
    proj_weight_grad = jnp.einsum(
        "tc,td->cd", normed_low, proj_full, preferred_element_type=jnp.float32
    )
    grad_normed = jnp.einsum(
        "td,cd->tc", proj_full, proj_weight, preferred_element_type=jnp.float32
    )
    frame_grad, input_gain_grad, input_bias_grad = norm_split_back(
        grad_normed, normal_in, scale_in, widen(input_gain)
    )
    terms = (
        input_gain_grad,
        input_bias_grad,
        proj_weight_grad,
        proj_bias_grad,
        conv_weight_grad,
        conv_bias_grad,
        encoder_gain_grad,
        encoder_bias_grad,
        attend_weight_grad,
        query_bias_grad,
        value_bias_grad,
        output_weight_grad,
        output_bias_grad,
        attend_gain_grad,
        attend_bias_grad,
        hidden_weight_grad,
        hidden_bias_grad,
        return_weight_grad,
        return_bias_grad,
        final_gain_grad,
        final_bias_grad,
    )
    return (result.astype(lowtype), frame_grad, terms)


def add_pairs(first, second):
    return tuple((left + right for left, right in zip(first, second)))


def per_device(
    features,
    lengths,
    input_gain,
    input_bias,
    proj_weight,
    proj_bias,
    conv_weight,
    conv_bias,
    encoder_gain,
    encoder_bias,
    attend_weight,
    query_bias,
    value_bias,
    output_weight,
    output_bias,
    attend_gain,
    attend_bias,
    hidden_weight,
    hidden_bias,
    return_weight,
    return_bias,
    final_gain,
    final_bias,
    out_grad,
):
    upstream_all = lax.all_to_all(out_grad[:, 0], "ch", split_axis=2, concat_axis=1, tiled=True)
    owned = None
    outputs = []
    frame_grads = []
    for micro in range(features.shape[0]):
        params = (
            lax.all_gather(input_gain, "rows", axis=0, tiled=True),
            lax.all_gather(input_bias, "rows", axis=0, tiled=True),
            lax.all_gather(proj_weight, "rows", axis=0, tiled=True),
            lax.all_gather(proj_bias, "rows", axis=0, tiled=True),
            lax.all_gather(conv_weight, "rows", axis=0, tiled=True),
            lax.all_gather(conv_bias, "rows", axis=0, tiled=True),
            lax.all_gather(encoder_gain, "rows", axis=0, tiled=True),
            lax.all_gather(encoder_bias, "rows", axis=0, tiled=True),
            lax.all_gather(attend_weight, "rows", axis=0, tiled=True),
            lax.all_gather(query_bias, "rows", axis=0, tiled=True),
            lax.all_gather(value_bias, "rows", axis=0, tiled=True),
            lax.all_gather(output_weight, "rows", axis=0, tiled=True),
            lax.all_gather(output_bias, "rows", axis=0, tiled=True),
            lax.all_gather(attend_gain, "rows", axis=0, tiled=True),
            lax.all_gather(attend_bias, "rows", axis=0, tiled=True),
            lax.all_gather(hidden_weight, "rows", axis=0, tiled=True),
            lax.all_gather(hidden_bias, "rows", axis=0, tiled=True),
            lax.all_gather(return_weight, "rows", axis=0, tiled=True),
            lax.all_gather(return_bias, "rows", axis=0, tiled=True),
            lax.all_gather(final_gain, "rows", axis=0, tiled=True),
            lax.all_gather(final_bias, "rows", axis=0, tiled=True),
        )
        result, frame_grad, terms = run_micro(
            features[micro, 0], upstream_all[micro], params, lengths[micro, 0]
        )
        outputs.append(result)
        frame_grads.append(frame_grad)
        shares = (
            lax.psum_scatter(terms[0], "rows", scatter_dimension=0, tiled=True),
            lax.psum_scatter(terms[1], "rows", scatter_dimension=0, tiled=True),
            lax.psum_scatter(terms[2], "rows", scatter_dimension=0, tiled=True),
            lax.psum_scatter(terms[3], "rows", scatter_dimension=0, tiled=True),
            lax.psum_scatter(terms[4], "rows", scatter_dimension=0, tiled=True),
            lax.psum_scatter(terms[5], "rows", scatter_dimension=0, tiled=True),
            lax.psum_scatter(terms[6], "rows", scatter_dimension=0, tiled=True),
            lax.psum_scatter(terms[7], "rows", scatter_dimension=0, tiled=True),
            lax.psum_scatter(terms[8], "rows", scatter_dimension=0, tiled=True),
            lax.psum_scatter(terms[9], "rows", scatter_dimension=0, tiled=True),
            lax.psum_scatter(terms[10], "rows", scatter_dimension=0, tiled=True),
            lax.psum_scatter(terms[11], "rows", scatter_dimension=0, tiled=True),
            lax.psum_scatter(terms[12], "rows", scatter_dimension=0, tiled=True),
            lax.psum_scatter(terms[13], "rows", scatter_dimension=0, tiled=True),
            lax.psum_scatter(terms[14], "rows", scatter_dimension=0, tiled=True),
            lax.psum_scatter(terms[15], "rows", scatter_dimension=0, tiled=True),
            lax.psum_scatter(terms[16], "rows", scatter_dimension=0, tiled=True),
            lax.psum_scatter(terms[17], "rows", scatter_dimension=0, tiled=True),
            lax.psum_scatter(terms[18], "rows", scatter_dimension=0, tiled=True),
            lax.psum_scatter(terms[19], "rows", scatter_dimension=0, tiled=True),
            lax.psum_scatter(terms[20], "rows", scatter_dimension=0, tiled=True),
        )
        owned = shares if owned is None else add_pairs(owned, shares)
    finished = lax.all_to_all(jnp.stack(outputs), "ch", split_axis=1, concat_axis=2, tiled=True)
    return (
        finished[:, None],
        jnp.stack(frame_grads)[:, None],
        owned[0],
        owned[1],
        owned[2],
        owned[3],
        owned[4],
        owned[5],
        owned[6],
        owned[7],
        owned[8],
        owned[9],
        owned[10],
        owned[11],
        owned[12],
        owned[13],
        owned[14],
        owned[15],
        owned[16],
        owned[17],
        owned[18],
        owned[19],
        owned[20],
    )


def solution(mesh):
    return jax.shard_map(
        per_device,
        mesh=mesh,
        in_specs=(
            P(None, "rows", None, "ch"),
            P(None, "rows"),
            P(("ch", "rows")),
            P(("ch", "rows")),
            P(("ch", "rows"), None),
            P(("ch", "rows")),
            P(("ch", "rows"), None, None),
            P(("ch", "rows")),
            P(("ch", "rows")),
            P(("ch", "rows")),
            P(("ch", "rows"), None),
            P(("ch", "rows")),
            P(("ch", "rows")),
            P(("ch", "rows"), None),
            P(("ch", "rows")),
            P(("ch", "rows")),
            P(("ch", "rows")),
            P(("ch", "rows"), None),
            P(("ch", "rows")),
            P(("ch", "rows"), None),
            P(("ch", "rows")),
            P(("ch", "rows")),
            P(("ch", "rows")),
            P(None, "rows", "ch", None),
        ),
        out_specs=(
            P(None, "rows", "ch", None),
            P(None, "rows", None, "ch"),
            P(("ch", "rows")),
            P(("ch", "rows")),
            P(("ch", "rows"), None),
            P(("ch", "rows")),
            P(("ch", "rows"), None, None),
            P(("ch", "rows")),
            P(("ch", "rows")),
            P(("ch", "rows")),
            P(("ch", "rows"), None),
            P(("ch", "rows")),
            P(("ch", "rows")),
            P(("ch", "rows"), None),
            P(("ch", "rows")),
            P(("ch", "rows")),
            P(("ch", "rows")),
            P(("ch", "rows"), None),
            P(("ch", "rows")),
            P(("ch", "rows"), None),
            P(("ch", "rows")),
            P(("ch", "rows")),
            P(("ch", "rows")),
        ),
        check_vma=False,
    )
```

profile of v0, /device:TPU:3, one launch (start us, length us, event | category | flops | bytes accessed | tf_op | source)
XLA Modules:
  0.0 1806.8 jit_solution(17812855597449714808)
XLA Ops:
  26.4 55.7 %all-reduce.59 = (bf16[192]{0:T(256)(128)(2,1)S(1)}, bf16[192]{0:T(256)(128)(2,1)S(1)}, bf16[128]{0:T(256)(128)(2,1)S(1)}, bf16[128]{0:T(256)(128)(2,1)S(1)}, bf...) all-reduce(bf16[192]{0:T(256)(128)(2,1)S(1)} %dynamic-update-slice., ...), channel_id=1, replica_groups=mesh['ch'=4,'rows'=32] {'rows'}, use_global_device_ids=true, to_apply=%add.10 | all-reduce | flops 3328 | bytes 13312
  82.2 37.8 %all-gather.8 = bf16[32,4,768]{2,1,0:T(4,128)(2,1)S(1)} all-gather(bf16[1,4,768]{2,1,0:T(4,128)(2,1)} %bitcast.847), channel_id=1, replica_groups=mesh['ch'=4,'rows'=32] {'rows'}, dimensions={0}, use_global_device_ids=true | all-gather | bytes 202752 | tf_op jit(solution)/shard_map/all_gather | solution.py:339
  138.3 25.3 %all-gather.9 = bf16[32,6,2304]{2,1,0:T(8,128)(2,1)S(1)} all-gather(bf16[1,6,2304]{2,1,0:T(8,128)(2,1)S(1)} %bitcast.769), channel_id=1, replica_groups=mesh['ch'=4,'rows'=32] {'rows'}, dimensions={0}, use_global_device_ids=true | all-gather | bytes 912384 | tf_op jit(solution)/shard_map/all_gather | solution.py:345
  167.4 44.2 %all-reduce.72.cloned.1.call-done = (f32[512,1,768]{0,1,2:T(1,128)}, f32[512,1,768]{0,1,2:T(1,128)}) async-done(((f32[512,1,768]{0,1,2:T(1,128)}, f32[512,1,768]{0,1,2:T(1,128)}), (f32[512,1,768]{0,1,2:T(1,128)}, f32[512,1,768]{0,1,2:T(1,128)})) %all-reduce.72.cloned.1.call-update) | async-done | bytes 3145744
  220.3 70.4 %while.73 = (s32[]{:T(128)}, f32[512,192]{0,1:T(8,128)}, bf16[192,48,128]{0,2,1:T(8,128)(2,1)}, bf16[640,192]{0,1:T(8,128)(2,1)S(1)}, s32[]{:T(128)}, /*index=5*...) while((s32[]{:T(128)}, f32[512,192]{0,1:T(8,128)}, ...), condition=%wide.region_31.32_spmd.clone, body=%wide.region_30.31_spmd.clone.sunk | while | flops 75694112 | bytes 10175100 | solution.py:85
  290.7 45.4 %while.72 = (s32[]{:T(128)}, f32[512,192]{0,1:T(8,128)S(1)}, bf16[192,48,128]{0,2,1:T(8,128)(2,1)}, bf16[640,192]{0,1:T(8,128)(2,1)S(1)}, s32[]{:T(128)}, /*inde...) while((s32[]{:T(128)}, f32[512,192]{0,1:T(8,128)S(1)}, ...), condition=%wide.region_6.7_spmd.clone, body=%wide.region_5.6_spmd.clone.sunk | while | flops 75694112 | bytes 10175100 | solution.py:85
  355.4 27.5 %all-gather.10 = bf16[32,6,768]{2,1,0:T(8,128)(2,1)S(1)} all-gather(bf16[1,6,768]{2,1,0:T(8,128)(2,1)S(1)} %bitcast.810), channel_id=1, replica_groups=mesh['ch'=4,'rows'=32] {'rows'}, dimensions={0}, use_global_device_ids=true | all-gather | bytes 304128 | tf_op jit(solution)/shard_map/all_gather | solution.py:348
  383.0 19.9 %reduce-scatter.13.cloned.1.call-done = f32[512,3,192]{0,2,1:T(8,128)} async-done(((f32[512,3,768]{0,2,1:T(8,128)}), f32[512,3,192]{0,2,1:T(8,128)}) %reduce-scatter.13.cloned.1.call-update) | async-done | bytes 1179664 | tf_op jit(solution)/shard_map/reduce_scatter | solution.py:27
  415.2 41.0 %reduce-scatter.17.cloned.1.call-done = f32[512,3,192]{0,2,1:T(8,128)} async-done(((f32[512,3,768]{0,2,1:T(8,128)}), f32[512,3,192]{0,2,1:T(8,128)}) %reduce-scatter.17.cloned.1.call-update) | async-done | bytes 1179664 | tf_op jit(solution)/shard_map/reduce_scatter | solution.py:27
  471.3 72.7 %all-reduce.70.cloned.1.call-done = (f32[512,1,768]{0,1,2:T(1,128)}, f32[512,1,768]{0,1,2:T(1,128)}) async-done(((f32[512,1,768]{0,1,2:T(1,128)}, f32[512,1,768]{0,1,2:T(1,128)}), (f32[512,1,768]{0,1,2:T(1,128)}, f32[512,1,768]{0,1,2:T(1,128)})) %all-reduce.70.cloned.1.call-update) | async-done | bytes 3145744
  565.6 59.3 %reduce-scatter.19.cloned.1.call-done = f32[512,1,768]{2,0,1:T(8,128)} async-done(((f32[512,1,3072]{2,0,1:T(8,128)}), f32[512,1,768]{2,0,1:T(8,128)}) %reduce-scatter.19.cloned.1.call-update) | async-done | bytes 1572880 | tf_op jit(solution)/shard_map/reduce_scatter | solution.py:27
  624.9 66.0 %reduce-scatter.15.cloned.1.call-done = f32[512,1,768]{2,0,1:T(8,128)} async-done(((f32[512,1,3072]{2,0,1:T(8,128)}), f32[512,1,768]{2,0,1:T(8,128)}) %reduce-scatter.15.cloned.1.call-update) | async-done | bytes 1572880 | tf_op jit(solution)/shard_map/reduce_scatter | solution.py:27
  737.4 59.1 %all-reduce.68.cloned.1.call-done = (f32[512,1,768]{0,1,2:T(1,128)}, f32[512,1,768]{0,1,2:T(1,128)}) async-done(((f32[512,1,768]{0,1,2:T(1,128)}, f32[512,1,768]{0,1,2:T(1,128)}), (f32[512,1,768]{0,1,2:T(1,128)}, f32[512,1,768]{0,1,2:T(1,128)})) %all-reduce.68.cloned.1.call-update) | async-done | bytes 3145744
  825.8 11.8 all-gather
  856.1 47.4 %all-gather.30.cloned.1.call-done = bf16[512,3072]{1,0:T(8,128)(2,1)} async-done(((bf16[512,768]{1,0:T(8,128)(2,1)}), bf16[512,3072]{1,0:T(8,128)(2,1)}) %all-gather.30.cloned.1.call-update) | async-done | bytes 3145744 | tf_op jit(solution)/shard_map/all_gather | solution.py:31
  907.9 37.0 %all-gather.28.cloned.1.call-done = bf16[512,3072]{1,0:T(8,128)(2,1)} async-done(((bf16[512,768]{1,0:T(8,128)(2,1)}), bf16[512,3072]{1,0:T(8,128)(2,1)}) %all-gather.28.cloned.1.call-update) | async-done | bytes 3145744 | tf_op jit(solution)/shard_map/all_gather | solution.py:31
  960.2 12.2 all-gather.6
  1018.9 31.7 %all-gather.24.cloned.1.call-done = bf16[512,3,768]{0,2,1:T(8,128)(2,1)} async-done(((bf16[512,3,192]{0,2,1:T(8,128)(2,1)}), bf16[512,3,768]{0,2,1:T(8,128)(2,1)}) %all-gather.24.cloned.1.call-update) | async-done | bytes 2359312 | tf_op jit(solution)/shard_map/all_gather | solution.py:31
  1069.8 176.2 %while.75 = (s32[]{:T(128)}, f32[192,48,128]{0,2,1:T(8,128)}, f32[512,192]{0,1:T(8,128)}, bf16[640,192]{0,1:T(8,128)(2,1)S(1)}, bf16[512,4,48]{0,2,1:T(8,128)(2,...) while((s32[]{:T(128)}, f32[192,48,128]{0,2,1:T(8,128)}, ...), condition=%wide.region_83.84_spmd.clone, body=%wide.region_82.83_spmd.clone.sunk | while | flops 151191616 | bytes 24331560 | solution.py:113
  1250.5 160.7 %while.74 = (s32[]{:T(128)}, f32[192,48,128]{0,2,1:T(8,128)}, f32[512,192]{0,1:T(8,128)}, bf16[640,192]{0,1:T(8,128)(2,1)S(1)}, bf16[512,4,48]{0,2,1:T(8,128)(2,...) while((s32[]{:T(128)}, f32[192,48,128]{0,2,1:T(8,128)}, ...), condition=%wide.region_64.65_spmd.clone, body=%wide.region_63.64_spmd.clone.sunk | while | flops 151191616 | bytes 24331560 | solution.py:113
  1413.9 11.9 all-gather.3
  1494.8 74.4 %fusion.325 = (f32[8,2304]{1,0:T(8,128)}, f32[8,768]{1,0:T(8,128)S(1)}, f32[8,3072]{1,0:T(8,128)S(1)}) fusion(f32[192,2304]{1,0:T(8,128)} %convolution_add_fusion, f32[192,768]{1,0:T(8,128)} %convolution_add_fusion.3, f32[192,3072]{1,0:T(8,128)S(1)} %convolution_add_fusion.1), kind=kCustom, calls=%all-reduce-scatter.3 | all-reduce-scatter fusion | flops 1572865 | bytes 4915712
  1614.1 104.1 %all-reduce.47 = (f32[128]{0:T(128)S(1)}, f32[128]{0:T(128)S(1)}, f32[192]{0:T(256)S(1)}, f32[192]{0:T(256)S(1)}, f32[192]{0:T(256)S(1)}, /*index=5*/f32[192]{0:...) all-reduce(f32[128]{0:T(128)S(1)} %add.1965, ...), channel_id=41, replica_groups=mesh['ch'=4,'rows'=32] {'rows'}, use_global_device_ids=true, to_apply=%region_89.90.clone | all-reduce | flops 3328 | bytes 26624
  1759.4 12.9 collective-permute-start.5
  (2112 shorter events, 919.6 us)
Async XLA Ops:
  8.0 203.7 %all-reduce.72.cloned.1.call-start = ((), (), s32[]{:S(2)}) async-start(), calls=%async_computation.24 | async-start | bytes 6291456
  137.0 78.3 %all-gather.20.cloned.1.call-start = ((), (), s32[]{:S(2)}) async-start(), calls=%async_computation.8 | async-start | bytes 2433024 | tf_op jit(solution)/shard_map/all_gather | solution.py:341
  137.5 265.3 %reduce-scatter.13.cloned.1.call-start = ((), (), s32[]{:S(2)}) async-start(), calls=%async_computation.9 | async-start | bytes 5898240 | tf_op jit(solution)/shard_map/reduce_scatter | solution.py:27
  350.1 106.0 %reduce-scatter.17.cloned.1.call-start = ((), (), s32[]{:S(2)}) async-start(), calls=%async_computation.12 | async-start | bytes 5898240 | tf_op jit(solution)/shard_map/reduce_scatter | solution.py:27
  353.3 115.6 %all-gather.32.cloned.1.call-start = ((), (), s32[]{:S(2)}) async-start(), calls=%async_computation.20 | async-start | bytes 1622016 | tf_op jit(solution)/shard_map/all_gather | solution.py:352
  353.9 190.1 %all-reduce.70.cloned.1.call-start = ((), (), s32[]{:S(2)}) async-start(), calls=%async_computation.23 | async-start | bytes 6291456
  468.2 156.7 %reduce-scatter.19.cloned.1.call-start = ((), (), s32[]{:S(2)}) async-start(), calls=%async_computation.13 | async-start | bytes 7864320 | tf_op jit(solution)/shard_map/reduce_scatter | solution.py:27
  559.3 131.6 %reduce-scatter.15.cloned.1.call-start = ((), (), s32[]{:S(2)}) async-start(), calls=%async_computation.10 | async-start | bytes 7864320 | tf_op jit(solution)/shard_map/reduce_scatter | solution.py:27
  564.6 135.0 %all-gather.22.cloned.1.call-start = ((), (), s32[]{:S(2)}) async-start(), calls=%async_computation.11 | async-start | bytes 1216512 | tf_op jit(solution)/shard_map/all_gather | solution.py:354
  565.2 231.4 %all-reduce.68.cloned.1.call-start = ((), (), s32[]{:S(2)}) async-start(), calls=%async_computation.22 | async-start | bytes 6291456
  723.7 179.8 %all-gather.30.cloned.1.call-start = ((), (), s32[]{:S(2)}) async-start(), calls=%async_computation.17 | async-start | bytes 3932160 | tf_op jit(solution)/shard_map/all_gather | solution.py:31
  855.1 89.8 %all-gather.28.cloned.1.call-start = ((), (), s32[]{:S(2)}) async-start(), calls=%async_computation.16 | async-start | bytes 3932160 | tf_op jit(solution)/shard_map/all_gather | solution.py:31
  855.8 159.9 %all-gather.26.cloned.1.call-start = ((), (), s32[]{:S(2)}) async-start(), calls=%async_computation.15 | async-start | bytes 2949120 | tf_op jit(solution)/shard_map/all_gather | solution.py:31
  979.0 71.6 %all-gather.24.cloned.1.call-start = ((), (), s32[]{:S(2)}) async-start(), calls=%async_computation.14 | async-start | bytes 2949120 | tf_op jit(solution)/shard_map/all_gather | solution.py:31
  999.0 799.1 %all-reduce.66.cloned.1.call-start = ((), (), s32[]{:S(2)}) async-start(), calls=%async_computation.21 | async-start | bytes 786432
  1439.3 360.2 %reduce-scatter.23.cloned.1.call-start = ((), (), s32[]{:S(2)}) async-start(), calls=%async_computation.19 | async-start | bytes 2433024 | tf_op jit(solution)/shard_map/reduce_scatter | solution.py:382
  1446.4 353.1 %reduce-scatter.21.cloned.1.call-start = ((), (), s32[]{:S(2)}) async-start(), calls=%async_computation.18 | async-start | bytes 4866048 | tf_op jit(solution)/shard_map/reduce_scatter | solution.py:369
  1569.2 37.2 %collective-permute-start.10 = (f32[8,768]{1,0:T(8,128)S(1)}, f32[8,768]{1,0:T(8,128)S(1)}, u32[]{:S(2)}, u32[]{:S(2)}) collective-permute-start(f32[8,768]{1,0:T(8,128)S(1)} %get-tuple-element.1183), channel_id=1, source_target_pairs={{0,3},{1,4},{2,5},{3,6},{4,7},{5,8},{6,9},{7,10},{8,11},{9,12},{10... | collective-permute-start | bytes 73736
  1571.2 38.0 %collective-permute-start.11 = (f32[8,768]{1,0:T(8,128)S(1)}, f32[8,768]{1,0:T(8,128)S(1)}, u32[]{:S(2)}, u32[]{:S(2)}) collective-permute-start(f32[8,768]{1,0:T(8,128)S(1)} %get-tuple-element.1183), channel_id=1, source_target_pairs={{0,4},{1,5},{2,6},{3,7},{4,8},{5,9},{6,10},{7,11},{8,12},{9,13},{1... | collective-permute-start | bytes 73736
  1580.1 146.8 %collective-permute-start.13 = (f32[8,768]{1,0:T(8,128)S(1)}, f32[8,768]{1,0:T(8,128)S(1)}, u32[]{:S(2)}, u32[]{:S(2)}) collective-permute-start(f32[8,768]{1,0:T(8,128)S(1)} %get-tuple-element.1183), channel_id=1, source_target_pairs={{0,6},{1,7},{2,8},{3,9},{4,10},{5,11},{6,12},{7,13},{8,14},{9,15},... | collective-permute-start | bytes 73736
  1601.0 129.4 %collective-permute-start.14 = (f32[8,768]{1,0:T(8,128)S(1)}, f32[8,768]{1,0:T(8,128)S(1)}, u32[]{:S(2)}, u32[]{:S(2)}) collective-permute-start(f32[8,768]{1,0:T(8,128)S(1)} %get-tuple-element.1183), channel_id=1, source_target_pairs={{0,7},{1,8},{2,9},{3,10},{4,11},{5,12},{6,13},{7,14},{8,15},{9,16}... | collective-permute-start | bytes 73736
  1606.4 126.0 %collective-permute-start.8 = (f32[8,768]{1,0:T(8,128)S(1)}, f32[8,768]{1,0:T(8,128)S(1)}, u32[]{:S(2)}, u32[]{:S(2)}) collective-permute-start(f32[8,768]{1,0:T(8,128)S(1)} %get-tuple-element.1183), channel_id=1, source_target_pairs={{0,1},{1,2},{2,3},{3,4},{4,5},{5,6},{6,7},{7,8},{8,9},{9,10},{10,1... | collective-permute-start | bytes 73736
  1609.2 127.8 %collective-permute-start.9 = (f32[8,768]{1,0:T(8,128)S(1)}, f32[8,768]{1,0:T(8,128)S(1)}, u32[]{:S(2)}, u32[]{:S(2)}) collective-permute-start(f32[8,768]{1,0:T(8,128)S(1)} %get-tuple-element.1183), channel_id=1, source_target_pairs={{0,2},{1,3},{2,4},{3,5},{4,6},{5,7},{6,8},{7,9},{8,10},{9,11},{10,... | collective-permute-start | bytes 73736
  1611.3 131.4 %collective-permute-start.7 = (f32[6,2304]{1,0:T(8,128)S(1)}, f32[6,2304]{1,0:T(8,128)S(1)}, u32[]{:S(2)}, u32[]{:S(2)}) collective-permute-start(f32[6,2304]{1,0:T(8,128)S(1)} %slice.60), channel_id=1, source_target_pairs={{0,8},{1,9},{2,10},{3,11},{4,12},{5,13},{6,14},{7,15},{8,16},{9,17... | collective-permute-start | bytes 165896
  (303 other events, 5800.2 us)
Sparse Core Ops, SparseCore 0:
  137.1 74.5 all-reduce.71
  350.2 52.6 reduce-scatter.12
  405.3 50.7 reduce-scatter.16
  468.3 75.6 all-reduce.69
  559.4 65.4 reduce-scatter.18
  627.2 63.6 reduce-scatter.14
  717.7 78.7 all-reduce.67
  855.2 48.2 all-gather.29
  905.2 39.7 all-gather.27
  979.1 36.6 all-gather.25
  1017.4 33.0 all-gather.23
Sparse Core Ops, SparseCore 1:
  139.7 43.1 all-gather.19
  356.0 44.9 all-gather.31
  567.4 44.7 all-gather.21
  1439.3 109.3 all-reduce.65
  1552.8 76.3 reduce-scatter.22
  1634.0 83.2 reduce-scatter.20
where the time goes:
time: 1820 us; the launch traced here: 1810 us
  waiting for transfers between devices  507 us (28%)
  blocking collectives  452 us (25%)
  local copies, waits for them, and re-layouts  409 us (22%)
  matrix products  156 us (9%)
  other arithmetic  146 us (8%)
  starting transfers between devices  102 us (6%)
  between operations  23 us (1%)
    unnamed x3, blocking collectives  234 us
    reduce_scatter x4, waiting for transfers between devices, sum_parts(): return lax.psum_scatter(terms, 'ch', scatter_dimension=2, tiled=True)  186 us
    unnamed x45, waiting for transfers between devices  184 us
    all_gather x4, waiting for transfers between devices, gather_full(): return lax.all_gather(slopes, 'ch', axis=2, tiled=True)  126 us
    dynamic_slice x64, local copies, waits for them, and re-layouts, tap_rows(): lax.dynamic_slice_in_dim(source, begin, rows, 0)  117 us
    unnamed x28, starting transfers between devices  93.3 us
    all_gather x6, blocking collectives, gather_full(): return lax.all_gather(slopes, 'ch', axis=2, tiled=True)  69.4 us
    unnamed x318, local copies, waits for them, and re-layouts  61.4 us
  transfers between devices with their start and end apart: 43, of which 17 were waited for; matrix products, arithmetic and copies ran while one was open for 12% of the time, Pallas kernels for 0%

commit v1 on v0

v1 whole, which is shorter than its diff:
```python
import jax
import jax.numpy as jnp
from jax import lax
from jax.sharding import PartitionSpec as P

HEAD_DIM = 64
EPS = 1e-05
NEGATIVE = -1000000000.0
FOLD = 16
ALL = ("ch", "rows")
LOW = jnp.bfloat16


def widen(values):
    return values.astype(jnp.float32)


def dot(left, right):
    return jnp.dot(left, right, preferred_element_type=jnp.float32)


def contract(spec, left, right):
    return jnp.einsum(spec, left, right, preferred_element_type=jnp.float32)


def smooth(values):
    return 0.5 * values * (1.0 + lax.erf(values * 0.7071067811865476))


def smooth_slope(values):
    return 0.5 * (1.0 + lax.erf(values * 0.7071067811865476)) + values * 0.3989422804014327 * jnp.exp(
        -0.5 * values * values
    )


def norm(values):
    mean = jnp.mean(values, axis=-1, keepdims=True)
    centred = values - mean
    scale = lax.rsqrt(jnp.mean(centred * centred, axis=-1, keepdims=True) + EPS)
    return centred * scale, scale


def norm_back(incoming, normal, scale, gain):
    scaled = incoming * gain
    first = jnp.mean(scaled, axis=-1, keepdims=True)
    second = jnp.mean(scaled * normal, axis=-1, keepdims=True)
    return scale * (scaled - first - normal * second)


def total(values):
    return jnp.sum(values.reshape(-1, values.shape[-1]), axis=0)


def fold_taps(turned, width, begin):
    span = turned.shape[-1] + width
    padded = jnp.pad(turned, [(0, 0)] * (turned.ndim - 1) + [(begin, width + FOLD - begin)])
    return jnp.stack([padded[..., j : j + span] for j in range(FOLD)], axis=2)


def per_device(
    features, lengths, input_gain, input_bias, proj_weight, proj_bias, conv_weight, conv_bias,
    encoder_gain, encoder_bias, attend_weight, query_bias, value_bias, output_weight, output_bias,
    attend_gain, attend_bias, hidden_weight, hidden_bias, return_weight, return_bias, final_gain,
    final_bias, out_grad,
):
    parts = lax.axis_size("ch")
    ranks = lax.axis_size("rows")
    here = lax.axis_index("ch")
    micros, _, frames, narrow = features.shape
    own = proj_bias.shape[0]
    width = proj_weight.shape[1]
    quarter = width // parts
    inner, taps = conv_weight.shape[1:]
    blocks = taps // FOLD
    groups = quarter // inner
    heads = quarter // HEAD_DIM
    hidden = hidden_weight.shape[1]
    deep = hidden // parts
    wide_in = narrow * parts
    own_in = input_gain.shape[0]
    own_hid = hidden_bias.shape[0]
    seg = out_grad.shape[2]

    small = jnp.stack(
        [proj_bias, conv_bias, encoder_gain, encoder_bias, query_bias, value_bias, output_bias,
         attend_gain, attend_bias, return_bias, final_gain, final_bias]
    )
    packed = jnp.concatenate([small.reshape(-1), input_gain, input_bias, hidden_bias])
    vectors = widen(lax.all_gather(packed, ALL, axis=0, tiled=False))
    count = small.shape[0]
    table = vectors[:, : count * own].reshape(-1, count, own).transpose(1, 0, 2).reshape(count, width)
    edge = count * own
    gain_in = vectors[:, edge : edge + own_in].reshape(-1)
    bias_in = vectors[:, edge + own_in : edge + 2 * own_in].reshape(-1)
    bias_hid = vectors[:, edge + 2 * own_in :].reshape(-1)
    mine = lax.dynamic_slice_in_dim(table, here * quarter, quarter, 1)
    proj_full = lax.all_gather(proj_weight, ALL, axis=0, tiled=True)
    folded = conv_weight.reshape(own, inner, blocks, FOLD).transpose(0, 2, 3, 1)
    folded = folded.reshape(own * blocks, FOLD * inner)
    conv_all = lax.all_gather(folded, "rows", axis=0, tiled=True)
    conv_all = conv_all.reshape(groups, inner, blocks, FOLD * inner).transpose(0, 2, 1, 3)
    conv_all = conv_all.reshape(groups, blocks * inner, FOLD * inner)
    mixed = jnp.concatenate(
        [
            attend_weight.reshape(own, 3, parts, quarter).transpose(2, 0, 1, 3).reshape(parts, own, 3 * quarter),
            output_weight.reshape(own, parts, quarter).transpose(1, 0, 2),
            hidden_weight.reshape(own, parts, deep).transpose(1, 0, 2),
        ],
        axis=2,
    )
    mixed = lax.all_to_all(mixed, "ch", split_axis=0, concat_axis=0, tiled=True)
    mixed = mixed.reshape(parts * own, -1)
    attend_all = lax.all_gather(mixed[:, : 3 * quarter], "rows", axis=0, tiled=True)
    attend_all = attend_all.reshape(ranks, parts, own, 3 * quarter).transpose(1, 0, 2, 3)
    attend_all = attend_all.reshape(width, 3 * quarter)
    mid = lax.all_gather(mixed[:, 3 * quarter :], ALL, axis=0, tiled=True)
    mid = mid.reshape(parts, ranks, parts, own, quarter + deep).transpose(2, 1, 3, 0, 4)
    mid = mid.reshape(width, parts, quarter + deep)
    output_full = mid[:, :, :quarter].reshape(width, width)
    hidden_full = mid[:, :, quarter:].reshape(width, hidden)
    return_full = lax.all_gather(return_weight, ALL, axis=0, tiled=True)

    live = jnp.arange(frames, dtype=jnp.int32)[None, :] < lengths
    keep = widen(live)[:, :, None]
    source = lax.all_gather(features[:, 0], "ch", axis=2, tiled=True)
    normal_in, scale_in = norm(widen(source))
    normed_low = (normal_in * gain_in + bias_in).astype(LOW)
    proj_mine = lax.dynamic_slice_in_dim(proj_full, here * quarter, quarter, 1)
    projected = (dot(normed_low, proj_mine) + mine[0]) * keep
    turned = projected.astype(LOW).transpose(0, 2, 1).reshape(micros, groups, inner, frames)
    spread = fold_taps(turned, taps, taps // 2)
    span = spread.shape[-1]
    spread = spread.reshape(micros, groups, FOLD * inner, span)
    sums = contract("gpk,mgku->mgpu", conv_all, spread)
    sums = sums.reshape(micros, groups, blocks, inner, span)
    conv = sum(sums[:, :, b, :, FOLD * b : FOLD * b + frames] for b in range(blocks))
    before = conv.reshape(micros, quarter, frames).transpose(0, 2, 1) + mine[1]
    summed = (projected + smooth(before)).astype(LOW)
    summed = lax.all_gather(summed, "ch", axis=2, tiled=True)

    normal_enc, scale_enc = norm(widen(summed))
    encoded = normal_enc * table[2] + table[3]
    encoded_low = encoded.astype(LOW)
    joint = dot(encoded_low, attend_all).reshape(micros, frames, 3, quarter)
    shape = (micros, frames, heads, HEAD_DIM)
    query = (joint[:, :, 0] + mine[4]).astype(LOW).reshape(shape)
    keys = joint[:, :, 1].astype(LOW).reshape(shape)
    value = (joint[:, :, 2] + mine[5]).astype(LOW).reshape(shape)
    ratio = HEAD_DIM ** (-0.5)
    scores = contract("mthd,mshd->mhts", query, keys) * ratio
    scores = jnp.where(live[:, None, None, :], scores, NEGATIVE)
    expo = jnp.exp(scores - jnp.max(scores, axis=-1, keepdims=True))
    probs = expo / jnp.sum(expo, axis=-1, keepdims=True)
    probs_low = probs.astype(LOW)
    context = contract("mhts,mshd->mthd", probs_low, value).astype(LOW)
    context = context.reshape(micros, frames, quarter)
    context = lax.all_to_all(context, "ch", split_axis=1, concat_axis=2, tiled=True)

    def mine_rows(values):
        return lax.dynamic_slice_in_dim(values, here * seg, seg, 1)

    attn_sum = mine_rows(encoded) + dot(context, output_full) + table[6]
    normal_att, scale_att = norm(attn_sum)
    attn_norm = normal_att * table[7] + table[8]
    attn_low = attn_norm.astype(LOW)
    pre_hidden = dot(attn_low, hidden_full) + bias_hid
    activated = smooth(pre_hidden).astype(LOW)
    ffn_sum = attn_norm + dot(activated, return_full) + table[9]
    normal_fin, scale_fin = norm(ffn_sum)
    output = (normal_fin * table[10] + table[11]).astype(LOW)
    upstream = widen(out_grad[:, 0])
    grad_ffn = norm_back(upstream, normal_fin, scale_fin, table[10])
    slope_outer = grad_ffn.astype(LOW)
    return_grad = contract("mtf,mtd->fd", activated, slope_outer)
    grad_act = contract("mtd,fd->mtf", slope_outer, return_full)
    slope_inner = (grad_act * smooth_slope(pre_hidden)).astype(LOW)
    hidden_grad = contract("mtc,mtf->cf", attn_low, slope_inner)
    grad_norm2 = grad_ffn + contract("mtf,cf->mtc", slope_inner, hidden_full)
    grad_attn = norm_back(grad_norm2, normal_att, scale_att, table[7])
    slope_att = grad_attn.astype(LOW)
    output_grad = contract("mtc,mtd->cd", context, slope_att)
    grad_context = contract("mtd,cd->mtc", slope_att, output_full).astype(LOW)

    return_share = lax.psum_scatter(return_grad.astype(LOW), ALL, scatter_dimension=0, tiled=True)
    middle = jnp.concatenate(
        [output_grad.reshape(width, parts, quarter), hidden_grad.reshape(width, parts, deep)], axis=2
    ).astype(LOW)
    middle = middle.reshape(parts, ranks, own, parts, quarter + deep).transpose(3, 1, 0, 2, 4)
    middle = middle.reshape(-1, quarter + deep)
    middle_share = lax.psum_scatter(middle, ALL, scatter_dimension=0, tiled=True)

    grad_context = lax.all_to_all(grad_context, "ch", split_axis=2, concat_axis=1, tiled=True)
    grad_context = grad_context.reshape(shape)
    grad_probs = contract("mthd,mshd->mhts", grad_context, value)
    grad_value = contract("mhts,mthd->mshd", probs_low, grad_context).astype(LOW)
    centre = jnp.sum(probs * grad_probs, axis=-1, keepdims=True)
    slope_scores = (probs * (grad_probs - centre)).astype(LOW)
    grad_query = (contract("mhts,mshd->mthd", slope_scores, keys) * ratio).astype(LOW)
    grad_key = (contract("mhts,mthd->mshd", slope_scores, query) * ratio).astype(LOW)
    flat = (micros, frames, quarter)
    slope_joint = jnp.concatenate(
        [grad_query.reshape(flat), grad_key.reshape(flat), grad_value.reshape(flat)], axis=2
    )
    attend_grad = contract("mtc,mtk->ck", encoded_low, slope_joint).astype(LOW)
    attend_grad = attend_grad.reshape(parts, ranks, own, 3 * quarter).transpose(1, 0, 2, 3)
    attend_share = lax.psum_scatter(
        attend_grad.reshape(-1, 3 * quarter), "rows", scatter_dimension=0, tiled=True
    )
    terms = contract("mtk,ck->mtc", slope_joint, attend_all).astype(LOW)
    terms = lax.psum_scatter(terms, "ch", scatter_dimension=1, tiled=True)
    grad_encoded = grad_attn + widen(terms)
    normal_own = mine_rows(normal_enc)
    grad_pos = norm_back(grad_encoded, normal_own, mine_rows(scale_enc), table[2])
    grad_pos = lax.all_to_all(grad_pos.astype(LOW), "ch", split_axis=2, concat_axis=1, tiled=True)

    grad_pos = widen(grad_pos)
    slope_conv = (grad_pos * smooth_slope(before)).astype(LOW)
    slope_turned = slope_conv.transpose(0, 2, 1).reshape(micros, groups, inner, frames)
    shifted = jnp.stack(
        [
            jnp.pad(slope_turned, ((0, 0), (0, 0), (0, 0), (FOLD * b, taps - FOLD * b)))
            for b in range(blocks)
        ],
        axis=2,
    ).reshape(micros, groups, blocks * inner, span)
    conv_grad = contract("mgpu,mgku->gpk", shifted, spread).astype(LOW)
    conv_grad = conv_grad.reshape(groups, blocks, inner, FOLD * inner).transpose(0, 2, 1, 3)
    conv_share = lax.psum_scatter(
        conv_grad.reshape(-1, FOLD * inner), "rows", scatter_dimension=0, tiled=True
    )
    back = contract("gpk,mgpu->mgku", conv_all, shifted)
    back = back.reshape(micros, groups, FOLD, inner, span)
    half = taps // 2
    conv_in = sum(back[:, :, j, :, half - j : half - j + frames] for j in range(FOLD))
    conv_in = conv_in.reshape(micros, quarter, frames).transpose(0, 2, 1)
    slope_proj = jnp.where(live[:, :, None], grad_pos + conv_in, 0.0).astype(LOW)
    slope_all = lax.all_gather(slope_proj, "ch", axis=2, tiled=True)
    grad_normed = contract("mtd,cd->mtc", slope_all, proj_full)
    source_grad = norm_back(grad_normed, normal_in, scale_in, gain_in)

    def mine_channels(values):
        return lax.dynamic_slice_in_dim(values, here * narrow, narrow, 2)

    features_grad = mine_channels(source_grad)
    proj_grad = contract("mtc,mtd->cd", mine_channels(normed_low), slope_all).astype(LOW)
    proj_share = lax.psum_scatter(proj_grad, "rows", scatter_dimension=0, tiled=True)

    whole = jnp.stack(
        [
            total(grad_encoded * normal_own), total(grad_encoded), total(widen(slope_att)),
            total(grad_norm2 * normal_att), total(grad_norm2), total(widen(slope_outer)),
            total(upstream * normal_fin), total(upstream),
        ]
    )
    whole = whole.reshape(8, -1, own).transpose(1, 0, 2).reshape(-1, 8 * own)
    whole = jnp.concatenate([whole, total(widen(slope_inner)).reshape(-1, own_hid)], axis=1)
    whole = lax.psum_scatter(whole, ALL, scatter_dimension=0, tiled=False)
    local = jnp.stack(
        [total(widen(slope_proj)), total(widen(slope_conv)), total(widen(grad_query).reshape(flat)),
         total(widen(grad_value).reshape(flat))]
    ).reshape(4, -1, own).transpose(1, 0, 2).reshape(-1, 4 * own)
    edges = mine_channels(grad_normed)
    local = jnp.concatenate(
        [
            local,
            total(edges * mine_channels(normal_in)).reshape(-1, own_in),
            total(edges).reshape(-1, own_in),
        ],
        axis=1,
    )
    local = lax.psum_scatter(local, "rows", scatter_dimension=0, tiled=False)

    share = jnp.concatenate([attend_share, middle_share], axis=1).reshape(parts, own, -1)
    share = lax.all_to_all(share, "ch", split_axis=0, concat_axis=0, tiled=True)
    share = widen(share)
    attend_share = share[:, :, : 3 * quarter].reshape(parts, own, 3, quarter).transpose(1, 2, 0, 3)
    output_share = share[:, :, 3 * quarter : 4 * quarter].transpose(1, 0, 2)
    hidden_share = share[:, :, 4 * quarter :].transpose(1, 0, 2)
    conv_share = widen(conv_share).reshape(own, blocks, FOLD, inner).transpose(0, 3, 1, 2)
    local_parts = [local[i * own : (i + 1) * own] for i in range(4)]
    whole_parts = [whole[i * own : (i + 1) * own] for i in range(8)]
    return (
        output[:, None],
        features_grad[:, None],
        local[4 * own : 4 * own + own_in],
        local[4 * own + own_in :],
        widen(proj_share),
        local_parts[0],
        conv_share.reshape(conv_weight.shape),
        local_parts[1],
        whole_parts[0],
        whole_parts[1],
        attend_share.reshape(attend_weight.shape),
        local_parts[2],
        local_parts[3],
        output_share.reshape(output_weight.shape),
        whole_parts[2],
        whole_parts[3],
        whole_parts[4],
        hidden_share.reshape(hidden_weight.shape),
        whole[8 * own :],
        widen(return_share),
        whole_parts[5],
        whole_parts[6],
        whole_parts[7],
    )


def solution(mesh):
    vector, matrix, cube = P(ALL), P(ALL, None), P(ALL, None, None)
    weights = (
        vector, vector, matrix, vector, cube, vector, vector, vector, matrix, vector, vector,
        matrix, vector, vector, vector, matrix, vector, matrix, vector, vector, vector,
    )
    by_channel = P(None, "rows", None, "ch")
    by_frame = P(None, "rows", "ch", None)
    return jax.shard_map(
        per_device,
        mesh=mesh,
        in_specs=(by_channel, P(None, "rows")) + weights + (by_frame,),
        out_specs=(by_frame, by_channel) + weights,
        check_vma=False,
    )
```

time: 1820 us -> 1180 us (0.65)
  local copies, waits for them, and re-layouts: 409 us -> 173 us
  blocking collectives: 452 us -> 325 us
  starting transfers between devices: 102 us -> 7.74 us
  other arithmetic: 146 us -> 54.3 us
  matrix products: 156 us -> 83.3 us
    dynamic_slice x128 -> x0, local copies, waits for them, and re-layouts: 178 us -> none  [the longest x64 117 us: tap_rows(): lax.dynamic_slice_in_dim(source, begin, rows, 0)]
    reduce_scatter x6 -> x3, waiting for transfers between devices: 186 us -> 359 us  [the longest x1 214 us: per_device(): lax.psum_scatter(return_grad.astype(LOW), ALL, scatter_dimension=0, tiled...]
    all_gather x7 -> x6, waiting for transfers between devices: 126 us -> 23.8 us  [the longest x1 21.2 us: per_device(): mid = lax.all_gather(mixed[:, 3 * quarter:], ALL, axis=0, tiled=True)]
    all_gather x9 -> x2, blocking collectives: 160 us -> 59 us  [the longest x1 34.2 us: per_device(): proj_full = lax.all_gather(proj_weight, ALL, axis=0, tiled=True)]
    unnamed x28 -> x3, starting transfers between devices: 93.3 us -> 0.13 us
    add x82 -> x2, other arithmetic: 98.7 us -> 9.66 us  [the longest x1 8.91 us: per_device(): sum((back[:, :, j, :, half - j:half - j + frames] for j in range(FOLD)))]
    dot_general x138 -> x23, matrix products: 156 us -> 77.5 us  [the longest x18 62.1 us: contract(): return jnp.einsum(spec, left, right, preferred_element_type=jnp.float32)]
    unnamed x45 -> x15, waiting for transfers between devices: 184 us -> 120 us
  transfers between devices with their start and end apart: 43 -> 14, of which waited for: 17 -> 8; matrix products, arithmetic and copies ran while one was open for 12% -> 18% of each run, Pallas kernels for 0% -> 0%
where the time goes in v1:
time: 1180 us; the launch traced here: 1170 us
  waiting for transfers between devices  511 us (43%)
  blocking collectives  325 us (28%)
  local copies, waits for them, and re-layouts  173 us (15%)
  matrix products  83.3 us (7%)
  other arithmetic  54.3 us (5%)
  between operations  17 us (1%)
    unnamed x3, blocking collectives  237 us
    reduce_scatter x1, waiting for transfers between devices, per_device(): lax.psum_scatter(return_grad.astype(LOW), ALL, scatter_dimension=0, tiled...  214 us
    unnamed x15, waiting for transfers between devices  120 us
    reduce_scatter x1, waiting for transfers between devices, per_device(): lax.psum_scatter(conv_grad.reshape(-1, FOLD * inner), 'rows', scatter_dim...  79.8 us
    reduce_scatter x1, waiting for transfers between devices, per_device(): lax.psum_scatter(middle, ALL, scatter_dimension=0, tiled=True)  65.3 us
    dot_general x18, matrix products, contract(): return jnp.einsum(spec, left, right, preferred_element_type=jnp.float32)  62.1 us
    all_gather x1, blocking collectives, per_device(): proj_full = lax.all_gather(proj_weight, ALL, axis=0, tiled=True)  34.2 us
    all_gather x1, blocking collectives, per_device(): lax.all_gather(mixed[:, :3 * quarter], 'rows', axis=0, tiled=True)  24.8 us
  transfers between devices with their start and end apart: 14, of which 8 were waited for; matrix products, arithmetic and copies ran while one was open for 18% of the time, Pallas kernels for 0%

profile of v1, /device:TPU:3, one launch (start us, length us, event | category | flops | bytes accessed | tf_op | source)
XLA Modules:
  0.0 1170.6 jit_solution(416390088307612346)
XLA Ops:
  12.6 67.5 %all-reduce.9 = bf16[13312]{0:T(1024)(128)(2,1)S(1)} all-reduce(bf16[13312]{0:T(1024)(128)(2,1)S(1)} %dynamic-update-slice), channel_id=3, replica_groups=mesh['ch'=4,'rows'=32] {'ch','rows'}, use_global_device_ids=true, to_apply=%add.9 | all-reduce | flops 13312 | bytes 53248
  81.3 34.2 %all-gather.2 = bf16[128,4,768]{2,1,0:T(4,128)(2,1)S(1)} all-gather(bf16[1,4,768]{2,1,0:T(4,128)(2,1)S(1)} %bitcast.476), channel_id=1, replica_groups=mesh['ch'=4,'rows'=32] {'ch','rows'}, dimensions={0}, use_global_device_ids=true | all-gather | bytes 792576 | tf_op jit(solution)/shard_map/all_gather | solution.py:97
  144.4 8.3 all_to_all.52
  161.5 24.8 %all_gather.36 = bf16[768,576]{1,0:T(8,128)(2,1)S(1)} all-gather(bf16[24,576]{1,0:T(8,128)(2,1)S(1)} %slice.411), channel_id=1, replica_groups=mesh['ch'=4,'rows'=32] {'rows'}, dimensions={0}, use_global_device_ids=true | all-gather | bytes 912384 | tf_op jit(solution)/shard_map/all_gather | solution.py:113
  220.2 21.2 %all-gather.14.cloned.1.call-done = bf16[3072,960]{1,0:T(8,128)(2,1)} async-done(((bf16[24,960]{1,0:T(8,128)(2,1)}), bf16[3072,960]{1,0:T(8,128)(2,1)}) %all-gather.14.cloned.1.call-update) | async-done | bytes 5898256 | tf_op jit(solution)/shard_map/all_gather | solution.py:116
  241.4 12.2 %reshape.518 = bf16[4,32,4,6,960]{4,3,2,1,0:T(8,128)(2,1)} reshape(bf16[3072,960]{1,0:T(8,128)(2,1)} %all-gather.14.cloned.1.call-done) | data formatting | bytes 11796480 | tf_op jit(solution)/shard_map/reshape | solution.py:117
  253.6 18.8 %copy.295 = bf16[4,32,6,4,960]{4,3,2,1,0:T(4,128)(2,1)} copy(bf16[4,32,6,4,960]{4,2,0,1,3:T(8,128)(2,1)} %bitcast.406) | data formatting | bytes 11796480 | tf_op jit(solution)/shard_map/transpose | solution.py:117
  275.5 9.7 slice.418
  287.9 9.4 reshape.582
  328.1 10.5 all_to_all.53
  358.8 22.2 %reduce-scatter.18.cloned.1.call-done = bf16[128,1536]{1,0:T(8,128)(2,1)} async-done(((bf16[512,1536]{1,0:T(8,128)(2,1)}), bf16[128,1536]{1,0:T(8,128)(2,1)}) %reduce-scatter.18.cloned.1.call-update) | async-done | bytes 393232
  387.0 9.5 all_to_all.54
  405.4 7.8 convolution_bitcast_fusion
  413.1 15.7 %copy.331 = f32[2,4,768,640]{3,2,1,0:T(8,128)} copy(f32[2,4,768,640]{2,3,0,1:T(8,128)} %convolution_bitcast_fusion) | data formatting | bytes 31457280 | tf_op jit(solution)/shard_map/gpk,mgpu->mgku/transpose | solution.py:23
  428.9 8.9 slice_add_fusion
  452.1 9.8 concatenate.32
  468.3 10.0 maximum_bitcast_fusion
  478.2 11.9 %reshape.541 = bf16[3072,960]{1,0:T(8,128)(2,1)} reshape(bf16[4,32,4,6,960]{4,3,2,1,0:T(8,128)(2,1)} %maximum_bitcast_fusion) | data formatting | bytes 11796480 | tf_op jit(solution)/shard_map/reshape | solution.py:189
  515.3 65.8 %all-reduce.12 = f32[128,72]{0,1:T(8,128)S(1)} all-reduce(f32[128,72]{0,1:T(8,128)S(1)} %pad_maximum_fusion.4), channel_id=8, replica_groups=mesh['ch'=4,'rows'=32] {'ch','rows'}, use_global_device_ids=true, to_apply=%region_38.39.clone | all-reduce | flops 9216 | bytes 73728
  588.9 104.1 %all-reduce.10 = f32[32,32]{0,1:T(8,128)S(1)} all-reduce(f32[32,32]{0,1:T(8,128)S(1)} %pad_maximum_fusion.5), channel_id=5, replica_groups=mesh['ch'=4,'rows'=32] {'rows'}, use_global_device_ids=true, to_apply=%region_26.27.clone | all-reduce | flops 1024 | bytes 8192
  695.8 65.3 %reduce-scatter.14.cloned.1.call-done = bf16[24,960]{1,0:T(8,128)(2,1)} async-done(((bf16[3072,960]{1,0:T(8,128)(2,1)}), bf16[24,960]{1,0:T(8,128)(2,1)}) %reduce-scatter.14.cloned.1.call-update) | async-done | bytes 46096 | tf_op jit(solution)/shard_map/reduce_scatter | solution.py:190
  766.0 96.9 %all-reduce.16.cloned.1.call-done = bf16[128,768]{1,0:T(8,128)(2,1)} async-done(((bf16[128,768]{1,0:T(8,128)(2,1)}), bf16[128,768]{1,0:T(8,128)(2,1)}) %all-reduce.16.cloned.1.call-update) | async-done | bytes 196624
  864.2 213.9 %reduce-scatter.16.cloned.1.call-done = bf16[24,768]{1,0:T(8,128)(2,1)} async-done(((bf16[3072,768]{1,0:T(8,128)(2,1)}), bf16[24,768]{1,0:T(8,128)(2,1)}) %reduce-scatter.16.cloned.1.call-update) | async-done | bytes 36880 | tf_op jit(solution)/shard_map/reduce_scatter | solution.py:184
  1079.5 79.8 %reduce-scatter.12.cloned.1.call-done = bf16[48,768]{1,0:T(8,128)(2,1)} async-done(((bf16[1536,768]{1,0:T(8,128)(2,1)}), bf16[48,768]{1,0:T(8,128)(2,1)}) %reduce-scatter.12.cloned.1.call-update) | async-done | bytes 73744 | tf_op jit(solution)/shard_map/reduce_scatter | solution.py:228
  (441 shorter events, 215.5 us)
Async XLA Ops:
  7.2 74.1 %copy-start.73 = (bf16[4,768]{1,0:T(4,128)(2,1)S(1)}, bf16[4,768]{1,0:T(4,128)(2,1)}, u32[]{:S(2)}) copy-start(bf16[4,768]{1,0:T(4,128)(2,1)} %param.28) | copy-start | bytes 18436
  7.2 108.6 %copy-start.79 = (s32[2,1]{0,1:T(1,128)S(1)}, s32[2,1]{0,1:T(1,128)}, u32[]{:S(2)}) copy-start(s32[2,1]{0,1:T(1,128)} %param.25) | copy-start | bytes 28
  7.2 109.3 %all-gather.20.cloned.1.call-start = ((), (), s32[]{:S(2)}) async-start(), calls=%async_computation.18 | async-start | bytes 1310720 | tf_op jit(solution)/shard_map/all_gather | solution.py:125
  7.9 123.1 %all-gather.10.cloned.1.call-start = ((), (), s32[]{:S(2)}) async-start(), calls=%async_computation.10 | async-start | bytes 2433024 | tf_op jit(solution)/shard_map/all_gather | solution.py:100
  9.9 178.7 %all-gather.12.cloned.1.call-start = ((), (), s32[]{:S(2)}) async-start(), calls=%async_computation.11 | async-start | bytes 1966080 | tf_op jit(solution)/shard_map/all_gather | solution.py:139
  80.5 42.1 %copy-start.53 = (f32[512]{0:T(512)}, f32[512]{0:T(512)S(1)}, u32[]{:S(2)}) copy-start(f32[512]{0:T(512)S(1)} %mul.306) | copy-start | bytes 6148
  143.9 97.5 %all-gather.14.cloned.1.call-start = ((), (), s32[]{:S(2)}) async-start(), calls=%async_computation.12 | async-start | bytes 6340608 | tf_op jit(solution)/shard_map/all_gather | solution.py:116
  153.5 155.5 %all-gather.16.cloned.1.call-start = ((), (), s32[]{:S(2)}) async-start(), calls=%async_computation.13 | async-start | bytes 4755456 | tf_op jit(solution)/shard_map/all_gather | solution.py:121
  158.3 34.1 %copy-start.59 = (f32[768]{0:T(1024)}, f32[768]{0:T(1024)S(1)}, u32[]{:S(2)}) copy-start(f32[768]{0:T(1024)S(1)} %add.356) | copy-start | bytes 9220
  204.3 14.1 %all-to-all-start.1 = ((bf16[2,512,192]{2,0,1:T(2,128)(2,1)}), bf16[2,512,192]{2,0,1:T(2,128)(2,1)S(1)}, u32[]{:S(2)}, u32[]{:S(2)}) async-start(bf16[2,512,192]{2,0,1:T(2,128)(2,1)} %copy.292), calls=%async_computation.1 | async-start | bytes 1048576 | tf_op jit(solution)/shard_map/all_to_all | solution.py:157
  207.8 173.2 %reduce-scatter.18.cloned.1.call-start = ((), (), s32[]{:S(2)}) async-start(), calls=%async_computation.19 | async-start | bytes 1966080
  357.5 132.8 %all-gather.18.cloned.1.call-start = ((), (), s32[]{:S(2)}) async-start(), calls=%async_computation.14 | async-start | bytes 1966080 | tf_op jit(solution)/shard_map/all_gather | solution.py:237
  438.8 257.0 %reduce-scatter.20.cloned.1.call-start = ((), (), s32[]{:S(2)}) async-start(), calls=%async_computation.21 | async-start | bytes 1013760
  445.6 315.5 %reduce-scatter.14.cloned.1.call-start = ((), (), s32[]{:S(2)}) async-start(), calls=%async_computation.16 | async-start | bytes 6340608 | tf_op jit(solution)/shard_map/reduce_scatter | solution.py:190
  490.2 372.6 %all-reduce.16.cloned.1.call-start = ((), (), s32[]{:S(2)}) async-start(), calls=%async_computation.20 | async-start | bytes 393216
  493.3 584.8 %reduce-scatter.16.cloned.1.call-start = ((), (), s32[]{:S(2)}) async-start(), calls=%async_computation.17 | async-start | bytes 4755456 | tf_op jit(solution)/shard_map/reduce_scatter | solution.py:184
  497.0 662.3 %reduce-scatter.12.cloned.1.call-start = ((), (), s32[]{:S(2)}) async-start(), calls=%async_computation.15 | async-start | bytes 2433024 | tf_op jit(solution)/shard_map/reduce_scatter | solution.py:228
  507.4 75.8 %copy-start = (bf16[2,1,512,512]{3,2,0,1:T(8,128)(2,1)S(1)}, bf16[2,1,512,512]{3,2,0,1:T(8,128)(2,1)}, u32[]{:S(2)}) copy-start(bf16[2,1,512,512]{3,2,0,1:T(8,128)(2,1)} %all-gather.20.cloned.1.call-done) | copy-start | bytes 3145732
  507.4 75.8 %copy-start.10 = (bf16[2,512,768]{1,2,0:T(8,128)(2,1)S(1)}, bf16[2,512,768]{1,2,0:T(8,128)(2,1)}, u32[]{:S(2)}) copy-start(bf16[2,512,768]{1,2,0:T(8,128)(2,1)} %all-gather.18.cloned.1.call-done) | copy-start | bytes 4718596
  507.4 75.8 %copy-start.38 = (f32[2,512]{1,0:T(2,128)S(1)}, f32[2,512]{1,0:T(2,128)}, u32[]{:S(2)}) copy-start(f32[2,512]{1,0:T(2,128)} %copy-done.37) | copy-start | bytes 12292
  507.4 75.8 %copy-start.40 = (f32[2,512]{1,0:T(2,128)S(1)}, f32[2,512]{1,0:T(2,128)}, u32[]{:S(2)}) copy-start(f32[2,512]{1,0:T(2,128)} %copy-done.39) | copy-start | bytes 12292
  507.4 75.8 %copy-start.54 = (f32[512]{0:T(512)S(1)}, f32[512]{0:T(512)}, u32[]{:S(2)}) copy-start(f32[512]{0:T(512)} %copy-done.53) | copy-start | bytes 6148
  508.5 74.3 %copy-start.16 = (bf16[2,512,192]{1,2,0:T(8,128)(2,1)S(1)}, bf16[2,512,192]{1,2,0:T(8,128)(2,1)}, u32[]{:S(2)}) copy-start(bf16[2,512,192]{1,2,0:T(8,128)(2,1)} %fusion.69) | copy-start | bytes 1179652
  762.6 398.5 %all-to-all-start.4 = ((bf16[4,6,1536]{2,1,0:T(8,128)(2,1)}), bf16[4,6,1536]{2,1,0:T(8,128)(2,1)S(1)}, u32[]{:S(2)}, u32[]{:S(2)}) async-start(bf16[4,6,1536]{2,1,0:T(8,128)(2,1)} %reshape.542), calls=%async_computation.6 | async-start | bytes 196608 | tf_op jit(solution)/shard_map/all_to_all | solution.py:274
  (78 other events, 442.3 us)
Sparse Core Ops, SparseCore 0:
  9.7 27.7 all-gather.19
  40.3 46.2 all-gather.9
  144.0 25.2 all-gather.11
  172.7 68.6 all-gather.13
  244.3 64.7 all-gather.15
  357.6 23.2 reduce-scatter.17
  438.9 27.7 all-gather.17
  470.3 73.7 reduce-scatter.19
  549.8 211.2 reduce-scatter.13
  764.2 98.6 all-reduce.15
  868.5 209.4 reduce-scatter.15
  1081.9 77.3 reduce-scatter.11

commit v2 on v1

v2 whole, which is shorter than its diff:
```python
import functools
import math

import jax
import jax.numpy as jnp
from jax import lax
from jax.experimental import pallas as pl
from jax.experimental.pallas import tpu as pltpu
from jax.sharding import PartitionSpec as P

HEAD_DIM = 64
EPS = 1e-05
NEGATIVE = -1000000000.0
FOLD = 16
ALL = ("ch", "rows")
LOW = jnp.bfloat16
MESH = pl.DeviceIdType.MESH
ROOM = 60 * 1024 * 1024


def widen(values):
    return values.astype(jnp.float32)


def dot(left, right):
    return jnp.dot(left, right, preferred_element_type=jnp.float32)


def contract(spec, left, right):
    return jnp.einsum(spec, left, right, preferred_element_type=jnp.float32)


def place(side):
    rank = lax.axis_index("rows")
    return {
        "y": lax.axis_index("ch"),
        "x": rank // (2 * side),
        "z": (rank // 2) % side,
        "k": rank % 2,
    }


def peer(spot, axis, step, sizes):
    moved = dict(spot)
    moved[axis] = (spot[axis] + step) % sizes[axis]
    return moved, (moved["y"], (moved["x"] * sizes["z"] + moved["z"]) * 2 + moved["k"])


def greet(targets):
    barrier = pltpu.get_barrier_semaphore()
    for target in targets:
        pl.semaphore_signal(barrier, inc=1, device_id=target, device_id_type=MESH)
    pl.semaphore_wait(barrier, len(targets))


def send(source, target, send_sem, recv_sem, device):
    copy = pltpu.make_async_remote_copy(
        src_ref=source, dst_ref=target, send_sem=send_sem, recv_sem=recv_sem,
        device_id=device, device_id_type=MESH,
    )
    copy.start()
    return copy


def whole(count):
    return [pl.BlockSpec(memory_space=pltpu.VMEM)] * count


def call_remote(kernel, shapes, ins, outs, scratch, ident, *values):
    return pl.pallas_call(
        kernel,
        out_shape=shapes,
        in_specs=ins,
        out_specs=outs,
        scratch_shapes=scratch,
        compiler_params=pltpu.CompilerParams(
            collective_id=ident, has_side_effects=True, vmem_limit_bytes=ROOM
        ),
    )(*values)


def over_ch(values, ident, mode, parts):
    block = values.shape if mode == "gather" else values.shape[1:]

    def kernel(in_ref, out_ref, held, send_sems, recv_sems):
        here = lax.axis_index("ch")
        others = [(here + step) % parts for step in range(1, parts)]
        rank = lax.axis_index("rows")
        greet([(other, rank) for other in others])
        copies = []
        for step, other in enumerate(others):
            source = in_ref if mode == "gather" else in_ref.at[other]
            target = held.at[step] if mode == "add" else out_ref.at[here]
            copies.append(
                send(source, target, send_sems.at[step], recv_sems.at[step], (other, rank))
            )
        if mode == "gather":
            out_ref[here] = in_ref[...]
        elif mode == "swap":
            out_ref[here] = in_ref[here]
        for copy in copies:
            copy.wait()
        if mode == "add":
            result = widen(in_ref[here])
            for step in range(parts - 1):
                result = result + widen(held[step])
            out_ref[...] = result

    shape = jax.ShapeDtypeStruct(
        block if mode == "add" else (parts,) + block,
        jnp.float32 if mode == "add" else values.dtype,
    )
    slots = (parts - 1,) + block if mode == "add" else (1, 16, 128)
    return call_remote(
        kernel, shape, whole(1), whole(1)[0],
        [
            pltpu.VMEM(slots, values.dtype),
            pltpu.SemaphoreType.DMA((parts - 1,)),
            pltpu.SemaphoreType.DMA((parts - 1,)),
        ],
        ident, values,
    )


def over_eight(blocks, pair, ident, parts):
    count = 2 * parts

    def kernel(block_ref, pair_ref, block_out, pair_out, send_sems, recv_sems):
        here, rank = lax.axis_index("ch"), lax.axis_index("rows")
        core = rank % 2
        mine = here * 2 + core
        base = rank - core
        steps = range(1, count)
        others = [(mine + step) % count for step in steps]
        devices = [(other // 2, base + other % 2) for other in others]
        greet(devices)
        copies = []
        for index, (other, device) in enumerate(zip(others, devices)):
            copies.append(
                send(block_ref.at[other], block_out.at[mine], send_sems.at[index],
                     recv_sems.at[index], device)
            )
        copies.append(
            send(pair_ref.at[1 - core], pair_out.at[core], send_sems.at[count - 1],
                 recv_sems.at[count - 1], (here, base + 1 - core))
        )
        block_out[mine] = block_ref[mine]
        pair_out[core] = pair_ref[core]
        for copy in copies:
            copy.wait()

    shapes = [jax.ShapeDtypeStruct(v.shape, v.dtype) for v in (blocks, pair)]
    return call_remote(
        kernel, shapes, whole(2), whole(2),
        [pltpu.SemaphoreType.DMA((count,)), pltpu.SemaphoreType.DMA((count,))],
        ident, blocks, pair,
    )


def job_copies(jobs, sizes):
    return sum(
        len(cuts) + sum(sizes[a] - 1 for order in orders for a in order)
        for _, cuts, orders in jobs
    )


def neighbours(jobs, spot, sizes):
    found = [peer(spot, "k", 1, sizes)[1]]
    for axis in ("y", "x", "z"):
        if any(axis in axes for axes, _, _ in jobs):
            found += [peer(spot, axis, step, sizes)[1] for step in range(1, sizes[axis])]
    return found


def window(axes, fixed, cut):
    lead = tuple(fixed.get(axis, slice(None)) for axis in axes)
    return lead + (pl.ds(cut[0], cut[1]), pl.ds(cut[2], cut[3]))


def gather_jobs(values, jobs, ident, sizes):
    total = job_copies(jobs, sizes)

    def kernel(*refs):
        count = len(jobs)
        ins, outs = refs[:count], refs[count : 2 * count]
        local, send_sems, recv_sems = refs[2 * count :]
        spot = place(sizes["z"])
        core = spot["k"]
        for number, (axes, _, _) in enumerate(jobs):
            pltpu.make_async_copy(
                ins[number],
                outs[number].at[(core,) + tuple(spot[a] for a in axes)],
                local.at[number],
            ).start()
        greet(neighbours(jobs, spot, sizes))
        for number, (axes, _, _) in enumerate(jobs):
            pltpu.make_async_copy(
                ins[number],
                outs[number].at[(core,) + tuple(spot[a] for a in axes)],
                local.at[number],
            ).wait()
        used = 0
        pending = []
        finished = []
        depth = max(len(axes) for axes, _, _ in jobs)
        waiting = {}
        for stage in range(depth + 1):
            for number, (axes, cuts, orders) in enumerate(jobs):
                for piece, (cut, order) in enumerate(zip(cuts, orders)):
                    if stage > len(order):
                        continue
                    for copy in waiting.pop((number, piece), []):
                        copy.wait_recv()
                    copies = []
                    if stage < len(order):
                        axis = order[stage]
                        fixed = {a: spot[a] for a in order[stage:]}
                        steps = range(1, sizes[axis])
                    else:
                        axis, fixed, steps = "k", {}, (1,)
                    view = outs[number].at[(core,) + window(axes, fixed, cut)]
                    for step in steps:
                        device = peer(spot, axis, step, sizes)[1]
                        copies.append(
                            send(view, view, send_sems.at[used], recv_sems.at[used], device)
                        )
                        used += 1
                    waiting[(number, piece)] = copies
                    finished += copies
        for copies in waiting.values():
            for copy in copies:
                copy.wait_recv()
        for copy in finished:
            copy.wait_send()

    shapes = [
        jax.ShapeDtypeStruct((2,) + tuple(sizes[a] for a in axes) + value.shape, value.dtype)
        for value, (axes, _, _) in zip(values, jobs)
    ]
    count = len(values)
    return call_remote(
        kernel, shapes, whole(count), whole(count),
        [
            pltpu.SemaphoreType.DMA((count,)),
            pltpu.SemaphoreType.DMA((total,)),
            pltpu.SemaphoreType.DMA((total,)),
        ],
        ident, *values,
    )


def loop_blocks(dims, body):
    count = math.prod(dims)
    if count == 1:
        body((0,) * len(dims))
        return

    def step(flat, carry):
        index = []
        rest = flat
        for size in reversed(dims):
            index.append(rest % size)
            rest = rest // size
        body(tuple(reversed(index)))
        return carry

    lax.fori_loop(0, count, step, 0)


def reduce_jobs(values, jobs, ident, sizes):
    total = job_copies(jobs, sizes)
    scratch = []
    layout = []
    for value, (axes, cuts, orders) in zip(values, jobs):
        for cut, order in zip(cuts, orders):
            block = (cut[1], cut[3])
            dims = tuple(sizes[a] for a in axes)
            entry = {"start": len(scratch)}
            scratch += [pltpu.VMEM(dims + block, LOW), pltpu.VMEM(dims + block, LOW)]
            left = list(axes)
            for axis in order:
                left.remove(axis)
                dims = tuple(sizes[a] for a in left)
                scratch.append(pltpu.VMEM((max(sizes[axis] - 1, 1),) + dims + block, LOW))
                if left:
                    scratch.append(pltpu.VMEM(dims + block, LOW))
            layout.append(entry)

    def kernel(*refs):
        count = len(jobs)
        ins, outs = refs[:count], refs[count : 2 * count]
        held = refs[2 * count : 2 * count + len(scratch)]
        local, send_sems, recv_sems = refs[2 * count + len(scratch) :]
        spot = place(sizes["z"])
        core = spot["k"]
        greet(neighbours(jobs, spot, sizes))
        used = 0
        finished = []
        states = []
        for number, (axes, cuts, orders) in enumerate(jobs):
            for cut, order in zip(cuts, orders):
                begin = layout[len(states)]["start"]
                arrived, summed = held[begin], held[begin + 1]
                cut_at = window(axes, {}, cut)
                copy = send(
                    ins[number].at[(1 - core,) + cut_at], arrived, send_sems.at[used],
                    recv_sems.at[used], peer(spot, "k", 1, sizes)[1],
                )
                mine = pltpu.make_async_copy(
                    ins[number].at[(core,) + cut_at], summed, local.at[len(states)]
                )
                mine.start()
                used += 1
                finished.append(copy)
                states.append(
                    {
                        "number": number, "axes": axes, "cut": cut, "order": order,
                        "next": begin + 2, "left": list(axes), "held": summed,
                        "arrived": arrived, "copies": [copy], "mine": mine,
                    }
                )
        depth = max(len(axes) for axes, _, _ in jobs)
        for stage in range(depth + 1):
            for state in states:
                order, left = state["order"], state["left"]
                if stage > len(order):
                    continue
                for copy in state["copies"]:
                    copy.wait_recv()
                cut = state["cut"]
                if stage == 0:
                    state["mine"].wait()
                    summed, arrived = state["held"], state["arrived"]

                    def pair(index, summed=summed, arrived=arrived):
                        summed[index] = summed[index] + arrived[index]

                    loop_blocks(tuple(sizes[a] for a in left), pair)
                else:
                    axis = order[stage - 1]
                    before, arrived = state["held"], state["arrived"]
                    spot_at = left.index(axis)
                    left.remove(axis)
                    rest = tuple(sizes[a] for a in left)
                    if left:
                        target = held[state["next"]]
                        state["next"] += 1
                    else:
                        target = None

                    def merge(
                        index, before=before, arrived=arrived, spot_at=spot_at, axis=axis,
                        target=target, cut=cut, number=state["number"], left=tuple(left),
                    ):
                        own = index[:spot_at] + (spot[axis],) + index[spot_at:] if left else (spot[axis],)
                        result = widen(before[own])
                        for step in range(sizes[axis] - 1):
                            result = result + widen(arrived[(step,) + (index if left else ())])
                        if target is None:
                            outs[number][cut[0] : cut[0] + cut[1], cut[2] : cut[2] + cut[3]] = result
                        else:
                            target[index] = result.astype(LOW)

                    loop_blocks(rest if left else (1,), merge)
                    state["held"] = target
                if stage < len(order):
                    axis = order[stage]
                    arrived = held[state["next"]]
                    state["next"] += 1
                    copies = []
                    for step in range(1, sizes[axis]):
                        moved, device = peer(spot, axis, step, sizes)
                        lead = tuple(
                            moved[axis] if a == axis else slice(None) for a in left
                        )
                        copies.append(
                            send(
                                state["held"].at[lead], arrived.at[step - 1],
                                send_sems.at[used], recv_sems.at[used], device,
                            )
                        )
                        used += 1
                    state["copies"] = copies
                    state["arrived"] = arrived
                    finished += copies
        for copy in finished:
            copy.wait_send()

    shapes = [jax.ShapeDtypeStruct(value.shape[-2:], jnp.float32) for value in values]
    count = len(values)
    pieces = len(layout)
    return call_remote(
        kernel, shapes, [pl.BlockSpec(memory_space=pl.ANY)] * count, whole(count),
        scratch
        + [
            pltpu.SemaphoreType.DMA((pieces,)),
            pltpu.SemaphoreType.DMA((total,)),
            pltpu.SemaphoreType.DMA((total,)),
        ],
        ident, *values,
    )


def smooth(values):
    return 0.5 * values * (1.0 + lax.erf(values * 0.7071067811865476))


def smooth_slope(values):
    return 0.5 * (1.0 + lax.erf(values * 0.7071067811865476)) + values * 0.3989422804014327 * jnp.exp(
        -0.5 * values * values
    )


def norm(values):
    mean = jnp.mean(values, axis=-1, keepdims=True)
    centred = values - mean
    scale = lax.rsqrt(jnp.mean(centred * centred, axis=-1, keepdims=True) + EPS)
    return centred * scale, scale


def norm_back(incoming, normal, scale, gain):
    scaled = incoming * gain
    first = jnp.mean(scaled, axis=-1, keepdims=True)
    second = jnp.mean(scaled * normal, axis=-1, keepdims=True)
    return scale * (scaled - first - normal * second)


def total(values):
    return jnp.sum(values.reshape(-1, values.shape[-1]), axis=0)


def fold_taps(turned, width, begin):
    span = turned.shape[-1] + width
    padded = jnp.pad(turned, [(0, 0)] * (turned.ndim - 1) + [(begin, width + FOLD - begin)])
    return jnp.stack([padded[..., j : j + span] for j in range(FOLD)], axis=2)


def unslab(count, parts, side):
    cells = jnp.arange(count, dtype=jnp.int32).reshape(parts, side * side, 2, -1)
    cells = cells.transpose(1, 0, 2, 3).reshape(1, count)
    return (jnp.arange(count, dtype=jnp.int32)[:, None] == cells).astype(LOW)


def ffn_grads(activated, slope_outer, inputs, slope_inner, context, slope_att, parts, slabs, tall):
    deep, frames = activated.shape[0] // parts, activated.shape[1]
    width = inputs.shape[0]
    half, eighth, thin = slope_outer.shape[1] // 2, deep // 2, width // (2 * parts)
    lanes = half + eighth + 128 * (-(-thin // 128))

    def kernel(act_ref, outer_ref, in_ref, inner_ref, ctx_ref, att_ref, out_ref):
        def put(left, right, begin, size):
            block = dot(left, right).astype(LOW)
            out_ref[0, 0, :, :, begin : begin + size] = block.reshape(slabs, tall, size)

        put(act_ref[...], outer_ref[...], 0, half)
        put(in_ref[...], inner_ref[...], half, eighth)
        put(ctx_ref[...], att_ref[0], half + eighth, lanes - half - eighth)

    return pl.pallas_call(
        kernel,
        grid=(2, parts),
        out_shape=jax.ShapeDtypeStruct((2, parts, slabs, tall, lanes), LOW),
        in_specs=[
            pl.BlockSpec((deep, frames), lambda k, c: (c, 0)),
            pl.BlockSpec((frames, half), lambda k, c: (0, k)),
            pl.BlockSpec((width, frames), lambda k, c: (0, 0)),
            pl.BlockSpec((frames, eighth), lambda k, c: (0, 2 * c + k)),
            pl.BlockSpec((width, frames), lambda k, c: (0, 0)),
            pl.BlockSpec((1, frames, lanes - half - eighth), lambda k, c: (2 * c + k, 0, 0)),
        ],
        out_specs=pl.BlockSpec((1, 1, slabs, tall, lanes), lambda k, c: (k, c, 0, 0, 0)),
        compiler_params=pltpu.CompilerParams(vmem_limit_bytes=ROOM),
    )(activated, slope_outer, inputs, slope_inner, context, slope_att)


def per_device(
    features, lengths, input_gain, input_bias, proj_weight, proj_bias, conv_weight, conv_bias,
    encoder_gain, encoder_bias, attend_weight, query_bias, value_bias, output_weight, output_bias,
    attend_gain, attend_bias, hidden_weight, hidden_bias, return_weight, return_bias, final_gain,
    final_bias, out_grad,
):
    parts = lax.axis_size("ch")
    ranks = lax.axis_size("rows")
    side = math.isqrt(ranks // 2)
    sizes = {"y": parts, "x": side, "z": side, "k": 2}
    here = lax.axis_index("ch")
    micros, _, frames, narrow = features.shape
    own = proj_bias.shape[0]
    width = proj_weight.shape[1]
    quarter = width // parts
    inner, taps = conv_weight.shape[1:]
    blocks = taps // FOLD
    groups = quarter // inner
    heads = quarter // HEAD_DIM
    hidden = hidden_weight.shape[1]
    wide_in = narrow * parts
    own_in = input_gain.shape[0]
    own_hid = hidden_bias.shape[0]
    seg = out_grad.shape[2]
    eight = 2 * parts
    squares = side * side
    tall = eight * own
    deep, thin, att = hidden // eight, width // eight, 3 * quarter // 2
    half = width // 2

    cut = jnp.concatenate(
        [
            hidden_weight.reshape(own, eight, deep),
            output_weight.reshape(own, eight, thin),
            attend_weight.reshape(own, 3, parts, quarter).transpose(0, 2, 1, 3).reshape(own, eight, att),
        ],
        axis=2,
    ).transpose(1, 0, 2)
    cut = jnp.pad(cut, ((0, 0), (0, -own % 16), (0, 0)))
    first = proj_weight.reshape(own_in, eight, thin).transpose(1, 0, 2).reshape(eight, 1, -1)
    lanes_cut = cut.shape[2]
    first = jnp.pad(first, ((0, 0), (0, 0), (0, -first.shape[2] % lanes_cut)))
    first = first.reshape(eight, -1, lanes_cut)
    first = jnp.pad(first, ((0, 0), (0, -first.shape[1] % 16), (0, 0)))
    cut = jnp.concatenate([cut, first], axis=1)
    tall_cut = own + -own % 16
    pair = return_weight.reshape(-1, 2, half).transpose(1, 0, 2)
    own_ret = pair.shape[1]
    pair = jnp.pad(pair, ((0, 0), (0, -own_ret % 16), (0, 0)))
    cut, pair = over_eight(cut, pair, 0, parts)
    first = cut[:, tall_cut:].reshape(eight, -1)[:, : own_in * thin].reshape(eight * own_in, thin)
    cut = cut[:, :own].reshape(tall, lanes_cut)
    pair = pair[:, :own_ret].reshape(2 * own_ret, half)
    slab = jnp.concatenate(
        [pair, cut[:, :deep], jnp.pad(cut[:, deep : deep + thin], ((0, 0), (0, -thin % 128)))], axis=1
    )
    everything = lax.all_gather(slab, ALL, axis=0, tiled=False)
    everything = everything.reshape(parts, squares, 2, tall, -1)

    small = jnp.stack(
        [proj_bias, conv_bias, encoder_gain, encoder_bias, query_bias, value_bias, output_bias,
         attend_gain, attend_bias, return_bias, final_gain, final_bias]
    )
    packed = jnp.concatenate([small.reshape(-1), input_gain, input_bias, hidden_bias])
    spare = 128 - thin
    vector_rows = -(-packed.shape[0] // spare)
    packed = jnp.pad(packed, (0, vector_rows * spare - packed.shape[0])).reshape(vector_rows, spare)
    packed = jnp.pad(packed, ((0, first.shape[0] - vector_rows), (0, 0)))
    early = jnp.concatenate([first, packed], axis=1)
    folded = conv_weight.reshape(own, inner, blocks, FOLD).transpose(0, 2, 3, 1)
    folded = folded.reshape(own * blocks, FOLD * inner)
    own_att = cut[:, deep + thin :]
    second = jnp.concatenate([folded, jnp.pad(own_att, ((0, 0), (0, -att % 128)))], axis=1)
    lanes_b = second.shape[1]
    split_b = lanes_b // 256 * 128
    cuts_b = [(0, tall, 0, split_b), (0, tall, split_b, lanes_b - split_b)]
    orders_b = [("z", "x"), ("x", "z")]
    early, second = gather_jobs(
        [early, second],
        [
            (("y", "x", "z"), [(0, early.shape[0], 0, 128)], [("z", "x", "y")]),
            (("x", "z"), cuts_b, orders_b),
        ],
        1, sizes,
    )
    early = early.reshape(2, parts, squares, -1, 128)
    vectors = early[:, :, :, :vector_rows, thin:].transpose(1, 2, 0, 3, 4)
    vectors = widen(vectors.reshape(parts * ranks, -1))
    count = small.shape[0]
    table = vectors[:, : count * own].reshape(-1, count, own).transpose(1, 0, 2).reshape(count, width)
    edge = count * own
    gain_in = vectors[:, edge : edge + own_in].reshape(-1)
    bias_in = vectors[:, edge + own_in : edge + 2 * own_in].reshape(-1)
    bias_hid = vectors[:, edge + 2 * own_in : edge + 2 * own_in + own_hid].reshape(-1)
    mine = lax.dynamic_slice_in_dim(table, here * quarter, quarter, 1)
    proj_full = early[..., :thin].transpose(2, 3, 1, 0, 4).reshape(wide_in, width)
    proj_full = dot(unslab(wide_in, parts, side), proj_full).astype(LOW)
    natural = unslab(width, parts, side)
    attend_all = second[..., FOLD * inner : FOLD * inner + att].reshape(2, width, att)
    attend_all = dot(natural, attend_all.transpose(1, 0, 2).reshape(width, 2 * att)).astype(LOW)
    conv_all = second[..., : FOLD * inner].reshape(2, squares, own, blocks, FOLD * inner)
    conv_all = conv_all.transpose(1, 0, 2, 3, 4).reshape(groups, inner, blocks, FOLD * inner)
    conv_all = conv_all.transpose(0, 2, 1, 3).reshape(groups, blocks * inner, FOLD * inner)

    live = jnp.arange(frames, dtype=jnp.int32)[None, :] < lengths
    keep = widen(live)[:, :, None]
    rows = micros * frames

    def join(gathered):
        return gathered.transpose(1, 0, 2).reshape(micros, frames, -1)

    source = join(over_ch(features.reshape(rows, narrow), 2, "gather", parts))
    normal_in, scale_in = norm(widen(source))
    normed_low = (normal_in * gain_in + bias_in).astype(LOW)
    proj_mine = lax.dynamic_slice_in_dim(proj_full, here * quarter, quarter, 1)
    projected = (dot(normed_low, proj_mine) + mine[0]) * keep
    turned = projected.astype(LOW).transpose(0, 2, 1).reshape(micros, groups, inner, frames)
    spread = fold_taps(turned, taps, taps // 2)
    span = spread.shape[-1]
    spread = spread.reshape(micros, groups, FOLD * inner, span)
    sums = contract("gpk,mgku->mgpu", conv_all, spread)
    sums = sums.reshape(micros, groups, blocks, inner, span)
    conv = sum(sums[:, :, b, :, FOLD * b : FOLD * b + frames] for b in range(blocks))
    before = conv.reshape(micros, quarter, frames).transpose(0, 2, 1) + mine[1]
    summed = (projected + smooth(before)).astype(LOW)
    summed = join(over_ch(summed.reshape(rows, quarter), 3, "gather", parts))

    normal_enc, scale_enc = norm(widen(summed))
    encoded = normal_enc * table[2] + table[3]
    encoded_low = encoded.astype(LOW)
    joint = dot(encoded_low, attend_all).reshape(micros, frames, 3, quarter)
    shape = (micros, frames, heads, HEAD_DIM)
    query = (joint[:, :, 0] + mine[4]).astype(LOW).reshape(shape)
    keys = joint[:, :, 1].astype(LOW).reshape(shape)
    value = (joint[:, :, 2] + mine[5]).astype(LOW).reshape(shape)
    ratio = HEAD_DIM ** (-0.5)
    scores = contract("mthd,mshd->mhts", query, keys) * ratio
    scores = jnp.where(live[:, None, None, :], scores, NEGATIVE)
    expo = jnp.exp(scores - jnp.max(scores, axis=-1, keepdims=True))
    probs = expo / jnp.sum(expo, axis=-1, keepdims=True)
    probs_low = probs.astype(LOW)
    context = contract("mhts,mshd->mthd", probs_low, value).astype(LOW)

    def to_frames(values):
        blocks_out = values.reshape(micros, parts, seg, quarter).transpose(1, 0, 2, 3)
        return blocks_out.reshape(parts, micros * seg, quarter)

    def to_channels(values):
        blocks_out = values.reshape(micros * seg, parts, quarter)
        return blocks_out.transpose(1, 0, 2)

    def from_frames(values):
        back = values.reshape(parts, micros, seg, quarter)
        return back.transpose(1, 0, 2, 3).reshape(micros, frames, quarter)

    context = over_ch(to_frames(context.reshape(micros, frames, quarter)), 4, "swap", parts)
    context = context.transpose(1, 0, 2).reshape(micros * seg, width)

    def mine_rows(values):
        picked = lax.dynamic_slice_in_dim(values, here * seg, seg, 1)
        return picked.reshape(micros * seg, values.shape[2])

    return_full = everything[..., :half].transpose(0, 1, 3, 2, 4).reshape(hidden, width)
    hidden_full = everything[..., half : half + deep].transpose(1, 3, 0, 2, 4).reshape(width, hidden)
    output_full = everything[..., half + deep : half + deep + thin].transpose(1, 3, 0, 2, 4)
    output_full = dot(natural, output_full.reshape(width, width)).astype(LOW)

    attn_sum = mine_rows(encoded) + dot(context, output_full) + table[6]
    normal_att, scale_att = norm(attn_sum)
    attn_norm = normal_att * table[7] + table[8]
    attn_low = dot(attn_norm.astype(LOW), natural).astype(LOW)
    pre_hidden = dot(attn_low, hidden_full) + bias_hid
    activated = smooth(pre_hidden).astype(LOW)
    ffn_sum = attn_norm + dot(activated, return_full) + table[9]
    normal_fin, scale_fin = norm(ffn_sum)
    output = (normal_fin * table[10] + table[11]).astype(LOW)
    upstream = widen(out_grad).reshape(micros * seg, width)
    grad_ffn = norm_back(upstream, normal_fin, scale_fin, table[10])
    slope_outer = grad_ffn.astype(LOW)
    grad_act = contract("td,fd->tf", slope_outer, return_full)
    slope_inner = (grad_act * smooth_slope(pre_hidden)).astype(LOW)
    hidden_nat = dot(natural, hidden_full).astype(LOW)
    grad_norm2 = grad_ffn + contract("tf,cf->tc", slope_inner, hidden_nat)
    grad_attn = norm_back(grad_norm2, normal_att, scale_att, table[7])
    slope_att = grad_attn.astype(LOW)
    grad_context = contract("td,cd->tc", slope_att, output_full).astype(LOW)
    att_cut = slope_att.reshape(micros * seg, eight, thin).transpose(1, 0, 2)
    att_cut = jnp.pad(att_cut, ((0, 0), (0, 0), (0, -thin % 128)))
    context_slab = contract("tc,cp->pt", context, natural).astype(LOW)
    ffn = ffn_grads(
        activated.T, slope_outer, attn_low.T, slope_inner, context_slab, att_cut, parts, squares, tall
    ).reshape(2, parts, side, side, tall, -1)

    grad_context = from_frames(over_ch(to_channels(grad_context), 5, "swap", parts)).reshape(shape)
    grad_probs = contract("mthd,mshd->mhts", grad_context, value)
    grad_value = contract("mhts,mthd->mshd", probs_low, grad_context).astype(LOW)
    centre = jnp.sum(probs * grad_probs, axis=-1, keepdims=True)
    slope_scores = (probs * (grad_probs - centre)).astype(LOW)
    grad_query = (contract("mhts,mshd->mthd", slope_scores, keys) * ratio).astype(LOW)
    grad_key = (contract("mhts,mthd->mshd", slope_scores, query) * ratio).astype(LOW)
    flat = (rows, quarter)
    slope_joint = jnp.concatenate(
        [grad_query.reshape(flat), grad_key.reshape(flat), grad_value.reshape(flat)], axis=1
    )
    encoded_slab = dot(encoded_low.reshape(rows, width), natural).astype(LOW)
    attend_grad = contract("tc,tk->ck", encoded_slab, slope_joint).astype(LOW)
    terms = contract("tk,ck->tc", slope_joint, attend_all).astype(LOW)
    terms = terms.reshape(micros, parts, seg, width).transpose(1, 0, 2, 3)
    terms = over_ch(terms.reshape(parts, micros * seg, width), 6, "add", parts)
    grad_encoded = grad_attn + terms
    normal_own = mine_rows(normal_enc)
    grad_pos = norm_back(grad_encoded, normal_own, mine_rows(scale_enc), table[2])
    grad_pos = widen(from_frames(over_ch(to_channels(grad_pos.astype(LOW)), 7, "swap", parts)))

    slope_conv = (grad_pos * smooth_slope(before)).astype(LOW)
    slope_turned = slope_conv.transpose(0, 2, 1).reshape(micros, groups, inner, frames)
    shifted = jnp.stack(
        [
            jnp.pad(slope_turned, ((0, 0), (0, 0), (0, 0), (FOLD * b, taps - FOLD * b)))
            for b in range(blocks)
        ],
        axis=2,
    ).reshape(micros, groups, blocks * inner, span)
    conv_grad = contract("mgpu,mgku->gpk", shifted, spread).astype(LOW)
    conv_grad = conv_grad.reshape(groups, blocks, inner, FOLD * inner).transpose(0, 2, 1, 3)
    conv_grad = conv_grad.reshape(squares, 2, tall, FOLD * inner).transpose(1, 0, 2, 3)
    back = contract("gpk,mgpu->mgku", conv_all, shifted)
    back = back.reshape(micros, groups, FOLD, inner, span)
    offset = taps // 2
    conv_in = sum(back[:, :, j, :, offset - j : offset - j + frames] for j in range(FOLD))
    conv_in = conv_in.reshape(micros, quarter, frames).transpose(0, 2, 1)
    slope_proj = jnp.where(live[:, :, None], grad_pos + conv_in, 0.0).astype(LOW)
    slope_all = join(over_ch(slope_proj.reshape(flat), 8, "gather", parts))
    grad_normed = contract("mtd,cd->mtc", slope_all, proj_full)
    source_grad = norm_back(grad_normed, normal_in, scale_in, gain_in)

    def mine_channels(values):
        return lax.dynamic_slice_in_dim(values, here * narrow, narrow, 2)

    features_grad = mine_channels(source_grad)
    proj_grad = contract("mtc,mtd->cd", mine_channels(normed_low), slope_all)

    full = jnp.stack(
        [
            total(grad_encoded * normal_own), total(grad_encoded), total(widen(slope_att)),
            total(grad_norm2 * normal_att), total(grad_norm2), total(widen(slope_outer)),
            total(upstream * normal_fin), total(upstream),
        ]
    )
    full = full.reshape(8, -1, own).transpose(1, 0, 2).reshape(-1, 8 * own)
    full = jnp.concatenate([full, total(widen(slope_inner)).reshape(-1, own_hid)], axis=1)
    full_count = full.shape[1]
    full = full.reshape(parts, squares, 2, 1, full_count).transpose(2, 0, 1, 3, 4).astype(LOW)
    full = jnp.pad(full, ((0, 0), (0, 0), (0, 0), (0, 15), (0, -full_count % 128)))
    full = full.reshape(2, parts, side, side, 16, -1)
    local = jnp.stack(
        [total(widen(slope_proj)), total(widen(slope_conv)), total(widen(grad_query).reshape(flat)),
         total(widen(grad_value).reshape(flat))]
    ).reshape(4, -1, own).transpose(1, 0, 2).reshape(-1, 4 * own)
    edges = mine_channels(grad_normed)
    local = jnp.concatenate(
        [
            local,
            total(edges * mine_channels(normal_in)).reshape(-1, own_in),
            total(edges).reshape(-1, own_in),
        ],
        axis=1,
    )
    local_count = local.shape[1]
    local = jnp.pad(local, ((0, 0), (0, width - local_count))).reshape(ranks, 1, width)
    local = jnp.concatenate([proj_grad.reshape(ranks, own_in, width), local], axis=1).astype(LOW)
    local = jnp.pad(local, ((0, 0), (0, -(own_in + 1) % 16), (0, 0)))
    local = local.reshape(squares, 2, -1, width).transpose(1, 0, 2, 3)
    local = local.reshape(2, side, side, -1, width)
    attend_grad = attend_grad.reshape(squares, tall, 2, att).transpose(2, 0, 1, 3)
    attend_grad = jnp.pad(attend_grad, ((0, 0), (0, 0), (0, 0), (0, -att % 128)))
    second_grad = jnp.concatenate([conv_grad, attend_grad], axis=3)
    second_grad = second_grad.reshape(2, side, side, tall, lanes_b)
    third = tall // 3
    lanes_a = ffn.shape[-1]
    ffn, full, second_grad, local = reduce_jobs(
        [ffn, full, second_grad, local],
        [
            (
                ("y", "x", "z"),
                [(i * third, third, 0, lanes_a) for i in range(3)],
                [("x", "z", "y"), ("z", "y", "x"), ("y", "x", "z")],
            ),
            (("y", "x", "z"), [(0, 16, 0, full.shape[-1])], [("y", "x", "z")]),
            (("x", "z"), cuts_b, orders_b),
            (("x", "z"), [(0, local.shape[-2], 0, width)], [("x", "z")]),
        ],
        9, sizes,
    )

    cut = jnp.concatenate(
        [ffn[:, half : half + deep], ffn[:, half + deep : half + deep + thin],
         second_grad[:, FOLD * inner : FOLD * inner + att]], axis=1
    ).reshape(eight, own, -1)
    cut = jnp.pad(cut, ((0, 0), (0, -own % 8), (0, 0)))
    cut, pair = over_eight(cut, ffn[:, :half].reshape(2, own_ret, half), 10, parts)
    cut = cut[:, :own].transpose(1, 0, 2)
    hidden_share = cut[:, :, :deep].reshape(hidden_weight.shape)
    output_share = cut[:, :, deep : deep + thin].reshape(output_weight.shape)
    attend_share = cut[:, :, deep + thin :].reshape(own, parts, 3, quarter).transpose(0, 2, 1, 3)
    return_share = pair.transpose(1, 0, 2).reshape(return_weight.shape)
    conv_share = second_grad[:, : FOLD * inner].reshape(own, blocks, FOLD, inner).transpose(0, 3, 1, 2)
    tail = local[own_in, :local_count]
    full = full[0, :full_count]
    local_parts = [tail[i * own : (i + 1) * own] for i in range(4)]
    full_parts = [full[i * own : (i + 1) * own] for i in range(8)]
    return (
        output.reshape(out_grad.shape),
        features_grad[:, None],
        tail[4 * own : 4 * own + own_in],
        tail[4 * own + own_in :],
        local[:own_in],
        local_parts[0],
        conv_share.reshape(conv_weight.shape),
        local_parts[1],
        full_parts[0],
        full_parts[1],
        attend_share.reshape(attend_weight.shape),
        local_parts[2],
        local_parts[3],
        output_share,
        full_parts[2],
        full_parts[3],
        full_parts[4],
        hidden_share,
        full[8 * own :],
        return_share,
        full_parts[5],
        full_parts[6],
        full_parts[7],
    )


def solution(mesh):
    vector, matrix, cube = P(ALL), P(ALL, None), P(ALL, None, None)
    weights = (
        vector, vector, matrix, vector, cube, vector, vector, vector, matrix, vector, vector,
        matrix, vector, vector, vector, matrix, vector, matrix, vector, vector, vector,
    )
    by_channel = P(None, "rows", None, "ch")
    by_frame = P(None, "rows", "ch", None)
    return jax.shard_map(
        per_device,
        mesh=mesh,
        in_specs=(by_channel, P(None, "rows")) + weights + (by_frame,),
        out_specs=(by_frame, by_channel) + weights,
        check_vma=False,
    )
```

time: 1180 us -> 640 us (0.54)
  waiting for transfers between devices: 511 us -> 0.02 us
  blocking collectives: 325 us -> 0 us
  Pallas kernels: 0 us -> 250 us
  local copies, waits for them, and re-layouts: 173 us -> 232 us
    reduce_scatter x3 -> x0, waiting for transfers between devices: 359 us -> none  [the longest x1 214 us: per_device(): lax.psum_scatter(return_grad.astype(LOW), ALL, scatter_dimension=0, tiled...]
    pallas_call x0 -> x12, Pallas kernels: none -> 250 us  [the longest x11 240 us: call_remote(): pl.pallas_call(kernel, out_shape=shapes, in_specs=ins, out_specs=outs, sc...]
    unnamed x3 -> x0, blocking collectives: 237 us -> none
    unnamed x15 -> x1, waiting for transfers between devices: 120 us -> 0.02 us
    all_gather x2 -> x0, blocking collectives: 59 us -> none  [the longest x1 34.2 us: per_device(): proj_full = lax.all_gather(proj_weight, ALL, axis=0, tiled=True)]
    unnamed x211 -> x213, local copies, waits for them, and re-layouts: 22.7 us -> 52.6 us
    all_to_all x3 -> x0, blocking collectives: 28.4 us -> none  [the longest x1 10.5 us: per_device(): lax.all_to_all(grad_context, 'ch', split_axis=2, concat_axis=1, tiled=True)]
    all_gather x6 -> x1, waiting for transfers between devices: 23.8 us -> 0.01 us  [per_device(): everything = lax.all_gather(slab, ALL, axis=0, tiled=False)]
  transfers between devices with their start and end apart: 14 -> 1, of which waited for: 8 -> 0; matrix products, arithmetic and copies ran while one was open for 18% -> 23% of each run, Pallas kernels for 0% -> 14%
where the time goes in v2:
time: 640 us; the launch traced here: 629 us
  Pallas kernels  250 us (39%)
  local copies, waits for them, and re-layouts  232 us (36%)
  matrix products  78.9 us (12%)
  other arithmetic  51.4 us (8%)
  between operations  16 us (2%)
    pallas_call x11, Pallas kernels, call_remote(): pl.pallas_call(kernel, out_shape=shapes, in_specs=ins, out_specs=outs, sc...  240 us
    dot_general x16, matrix products, contract(): return jnp.einsum(spec, left, right, preferred_element_type=jnp.float32)  61.4 us
    unnamed x213, local copies, waits for them, and re-layouts  52.6 us
    transpose x1, local copies, waits for them, and re-layouts, contract(): return jnp.einsum(spec, left, right, preferred_element_type=jnp.float32)  16.1 us
    convert_element_type x7, local copies, waits for them, and re-layouts, widen(): return values.astype(jnp.float32)  14.4 us
  transfers between devices with their start and end apart: 1, of which 0 were waited for; matrix products, arithmetic and copies ran while one was open for 23% of the time, Pallas kernels for 14%

profile of v2, /device:TPU:3, one launch (start us, length us, event | category | flops | bytes accessed | tf_op | source)
XLA Modules:
  0.0 629.2 jit_solution(8187119196153421190)
XLA Ops:
  13.0 11.6 %shard_map.411 = (bf16[8,32,768]{2,1,0:T(8,128)(2,1)}, bf16[2,32,384]{2,1,0:T(8,128)(2,1)}) custom-call(bf16[8,32,768]{2,1,0:T(8,128)(2,1)} %fusion.148.block_ref, bf16[2,32,384]{2,1,0:T(8,128)(2,1)} %pad.96.pair_ref), custom_call_target="tpu_custom_call" | custom-call | tf_op jit(solution)/shard_map/pallas_call | solution.py:70
  33.3 29.8 %shard_map.412 = (bf16[2,4,4,4,32,128]{5,4,3,2,1,0:T(8,128)(2,1)}, bf16[2,4,4,48,1152]{4,3,2,1,0:T(8,128)(2,1)}) custom-call(bf16[32,128]{1,0:T(8,128)(2,1)} %fusion.168.refs_0_, bf16[48,1152]{1,0:T(8,128)(2,1)} %fusion.159.refs_1_), custom_call_target="tpu_custom_call" | custom-call | tf_op jit(solution)/shard_map/pallas_call | solution.py:70
  73.1 18.8 %shard_map.410 = bf16[4,1024,128]{2,1,0:T(8,128)(2,1)} custom-call(bf16[1024,128]{1,0:T(8,128)(2,1)} %bitcast.575), custom_call_target="tpu_custom_call" | custom-call | tf_op jit(solution)/shard_map/pallas_call | solution.py:70
  129.3 7.1 %copy.299 = bf16[2,4,16,48,640]{4,3,2,0,1:T(8,128)(2,1)} copy(bf16[2,4,16,48,640]{4,3,1,0,2:T(8,128)(2,1)} %fusion.146) | data formatting | bytes 15728640 | tf_op jit(solution)/shard_map/stack | solution.py:435
  136.5 6.0 fusion.192
  146.9 28.8 %shard_map.413 = bf16[4,1024,192]{2,1,0:T(8,128)(2,1)} custom-call(bf16[1024,192]{1,0:T(8,128)(2,1)} %bitcast.537), custom_call_target="tpu_custom_call" | custom-call | tf_op jit(solution)/shard_map/pallas_call | solution.py:70
  229.2 6.9 %fusion.186 = (f32[2,3,512]{2,1,0:T(4,128)}, f32[2,3,512,512]{2,3,1,0:T(8,128)}) fusion(pred[2,512]{1,0:T(4,128)(4,1)} %get-tuple-element.205, bf16[2,512,3,64]{1,3,2,0:T(8,128)(2,1)} %bitcast.549, f32[2,512,3,64]{1,3,2,0:T(8,128)} %bitcast.531, f32[3,64]{1,0:T(4,128)} %add.441), kind=kOutput, calls=%fused_computation.349 | convolution fusion | flops 208011776 | bytes 7485184 | tf_op jit(solution)/shard_map/sub | solution.py:614
  244.6 10.8 %shard_map.414 = bf16[4,256,192]{2,1,0:T(8,128)(2,1)} custom-call(bf16[4,256,192]{2,1,0:T(8,128)(2,1)} %bitcast.540), custom_call_target="tpu_custom_call" | custom-call | tf_op jit(solution)/shard_map/pallas_call | solution.py:70
  265.9 8.4 %fusion.180 = (bf16[4,16,2,48,384]{4,3,2,1,0:T(8,128)(2,1)}, bf16[4,16,2,48,384]{4,3,2,1,0:T(8,128)(2,1)}) fusion(bf16[4,16,2,48,896]{4,3,2,1,0:T(8,128)(2,1)} %bitcast.505), kind=kLoop, calls=%fused_computation.343 | loop fusion | bytes 18874368 | tf_op jit(solution)/shard_map/slice | solution.py:638
  274.2 8.3 %copy.424 = bf16[4,16,2,48,384]{4,2,3,1,0:T(2,128)(2,1)} copy(bf16[4,16,2,48,384]{4,3,2,1,0:T(8,128)(2,1)} %get-tuple-element.165) | data formatting | bytes 9437184
  294.4 9.2 %copy.468 = bf16[4,16,2,48,384]{4,2,0,3,1:T(2,128)(2,1)} copy(bf16[4,16,2,48,384]{4,3,2,1,0:T(8,128)(2,1)} %get-tuple-element.166) | data formatting | bytes 9437184
  303.6 11.4 %reshape.905 = bf16[768,3072]{1,0:T(8,128)(2,1)} reshape(bf16[16,48,4,2,384]{4,3,2,1,0:T(2,128)(2,1)} %bitcast.501) | data formatting | bytes 9437184 | tf_op jit(solution)/shard_map/reshape | solution.py:639
  327.6 9.5 %multiply_reduce_fusion.2 = (bf16[768]{0:T(1024)(128)(2,1)S(1)}, f32[256]{0:T(256)S(1)}, f32[256]{0:T(256)S(1)}, bf16[768]{0:T(1024)(128)(2,1)}, f32[256,768]{1,0:T(8,128)}) fusion(f32[256,768]{1,0:T(8,128)S(1)} %get-tuple-element.212, f32[256]{0:T(256)S(1)} %copy-done.67, f32[256]{0:T(256)S(1)} %copy-done.57, f32[768]{0:T(1024)S(1)} %copy-done.38, ...), kind=kOutput, calls=%fused_computation.187 | convolution fusion | flops 4836751360 | bytes 8664064 | tf_op jit(solution)/shard_map/tf,cf->tc/dot_general | solution.py:30
  340.4 11.2 %shard_map.415 = bf16[4,256,192]{2,1,0:T(8,128)(2,1)} custom-call(bf16[4,256,192]{2,1,0:T(8,128)(2,1)} %bitcast.542), custom_call_target="tpu_custom_call" | custom-call | tf_op jit(solution)/shard_map/pallas_call | solution.py:70
  370.2 23.0 %shard_map.416 = f32[256,768]{1,0:T(8,128)} custom-call(bf16[4,256,768]{2,1,0:T(8,128)(2,1)} %bitcast.516), custom_call_target="tpu_custom_call" | custom-call | tf_op jit(solution)/shard_map/pallas_call | solution.py:70
  396.8 10.8 %shard_map.417 = bf16[4,256,192]{2,1,0:T(8,128)(2,1)} custom-call(bf16[4,256,192]{2,1,0:T(8,128)(2,1)} %bitcast.544), custom_call_target="tpu_custom_call" | custom-call | tf_op jit(solution)/shard_map/pallas_call | solution.py:70
  412.3 9.9 %bitcast_convert_fusion = bf16[4,384,768]{2,1,0:T(8,128)(2,1)} fusion(bf16[2,4,384,640]{3,2,1,0:T(8,128)(2,1)S(1)} %bitcast.521, bf16[2,4,768,640]{3,2,0,1:T(8,128)(2,1)} %bitcast.513), kind=kOutput, calls=%fused_computation.19 | convolution fusion | flops 3021078528 | bytes 14155776 | tf_op jit(solution)/shard_map/mgpu,mgku->gpk/dot_general | solution.py:30
  422.2 7.8 %convolution_bitcast_fusion = f32[2,4,768,640]{2,3,0,1:T(8,128)} fusion(bf16[4,384,768,1]{2,1,3,0:T(8,128)(2,1)S(1)} %bitcast.510, bf16[2,4,384,640]{3,2,1,0:T(8,128)(2,1)S(1)} %bitcast.522), kind=kOutput, calls=%fused_computation.1 | convolution fusion | flops 3019898880 | bytes 22020096 | tf_op jit(solution)/shard_map/gpk,mgpu->mgku/dot_general | solution.py:30
  429.9 16.1 %copy.355 = f32[2,4,768,640]{3,2,1,0:T(8,128)} copy(f32[2,4,768,640]{2,3,0,1:T(8,128)} %convolution_bitcast_fusion) | data formatting | bytes 31457280 | tf_op jit(solution)/shard_map/gpk,mgpu->mgku/transpose | solution.py:30
  446.1 8.8 %slice_add_fusion = f32[2,4,1,48,512]{4,3,2,1,0:T(8,128)S(1)} fusion(f32[2,4,16,48,640]{4,3,2,1,0:T(8,128)} %bitcast.490), kind=kLoop, calls=%fused_computation.132 | loop fusion | flops 2949120 | bytes 13369344 | tf_op jit(solution)/shard_map/add | solution.py:705
  482.9 28.5 %shard_map.418 = bf16[4,1024,192]{2,1,0:T(8,128)(2,1)} custom-call(bf16[1024,192]{1,0:T(8,128)(2,1)} %bitcast.536), custom_call_target="tpu_custom_call" | custom-call | tf_op jit(solution)/shard_map/pallas_call | solution.py:70
  527.4 10.7 %shard_map.419 = bf16[2,4,16,48,896]{4,3,2,1,0:T(8,128)(2,1)} custom-call(bf16[3072,256]{1,0:T(8,128)(2,1)} %copy.361.act_ref, bf16[256,768]{1,0:T(8,128)(2,1)} %copy-done.21, bf16[768,256]{1,0:T(8,128)(2,1)} %bitcast.571, bf16[256,3072]{1,0:T(8,128)(2,1)} %get-tuple-element.222.inner_ref, bf16[768,256]{1,0:T(8,128)(2,1)} %fusion.59.ctx_ref, ...), custom_call_target="tpu_custom_call" | custom-call | tf_op jit(solution)/shard_map/pallas_call | solution.py:459
  538.1 58.3 %shard_map.420 = (f32[48,896]{1,0:T(8,128)}, f32[16,128]{1,0:T(8,128)}, f32[48,1152]{1,0:T(8,128)}, f32[16,768]{1,0:T(8,128)}) custom-call(bf16[2,4,4,4,48,896]{5,4,3,2,1,0:T(8,128)(2,1)} %bitcast.491, bf16[2,4,4,4,16,128]{5,4,3,2,1,0:T(8,128)(2,1)} %bitcast.538, bf16[2,4,4,48,1152]{4,3,2,1,0:T(8,128)(2,1)} %bitcast.502, bf16[2,4,4,16,768]{4,3,2,1,0:T(8,128)(2,1)} %bitcast.534), custom_call_target="tpu_custom_call" | custom-call | tf_op jit(solution)/shard_map/pallas_call | solution.py:70
  608.4 7.9 %shard_map.421 = (f32[8,8,768]{2,1,0:T(8,128)}, f32[2,24,384]{2,1,0:T(8,128)}) custom-call(f32[8,8,768]{2,1,0:T(8,128)} %pad.115.block_ref, f32[2,24,384]{2,1,0:T(8,128)} %bitcast.574), custom_call_target="tpu_custom_call" | custom-call | tf_op jit(solution)/shard_map/pallas_call | solution.py:70
  (469 shorter events, 253.5 us)
Async XLA Ops:
  7.2 257.2 %all-gather.3.cloned.1.call-start = ((), (), s32[]{:S(2)}) async-start(), calls=%async_computation | async-start | bytes 11096064 | tf_op jit(solution)/shard_map/all_gather | solution.py:532
  95.1 15.0 %copy-start.33 = (f32[2,512]{1,0:T(2,128)}, f32[2,512]{1,0:T(2,128)S(1)}, u32[]{:S(2)}) copy-start(f32[2,512]{1,0:T(2,128)S(1)} %rsqrt.47) | copy-start | bytes 12292
  108.1 28.3 %copy-start.2 = (bf16[4,8,48,768]{3,2,1,0:T(8,128)(2,1)}, bf16[4,8,48,768]{3,2,1,0:T(8,128)(2,1)S(1)}, u32[]{:S(2)}) copy-start(bf16[4,8,48,768]{3,2,1,0:T(8,128)(2,1)S(1)} %copy.301) | copy-start | bytes 7077892
  108.9 35.9 %copy-start.54 = (f32[1,192]{1,0:T(1,128)}, f32[1,192]{1,0:T(1,128)S(1)}, u32[]{:S(2)}) copy-start(f32[1,192]{1,0:T(1,128)S(1)} %get-tuple-element.195) | copy-start | bytes 2308
  146.9 33.7 %copy-start.9 = (bf16[2,1,128,768]{3,2,1,0:T(8,128)(2,1)S(1)}, bf16[2,1,128,768]{3,2,1,0:T(8,128)(2,1)}, u32[]{:S(2)}) copy-start(bf16[2,1,128,768]{3,2,1,0:T(8,128)(2,1)} %param.47) | copy-start | bytes 1179652
  175.8 8.7 %copy-start.42 = (f32[1,128,6]{1,2,0:T(8,128)S(1)}, f32[1,128,6]{1,2,0:T(8,128)}, u32[]{:S(2)}) copy-start(f32[1,128,6]{1,2,0:T(8,128)} %get-tuple-element.191) | copy-start | bytes 9220
  175.8 9.5 %copy-start.41 = (f32[1,128,6]{1,2,0:T(8,128)S(1)}, f32[1,128,6]{1,2,0:T(8,128)}, u32[]{:S(2)}) copy-start(f32[1,128,6]{1,2,0:T(8,128)} %get-tuple-element.192) | copy-start | bytes 9220
  175.8 10.4 %copy-start.29 = (f32[128,24]{1,0:T(8,128)S(1)}, f32[128,24]{1,0:T(8,128)}, u32[]{:S(2)}) copy-start(f32[128,24]{1,0:T(8,128)} %slice.506) | copy-start | bytes 36868
  175.8 11.1 %copy-start.75 = (f32[192]{0:T(256)S(1)}, f32[192]{0:T(256)}, u32[]{:S(2)}) copy-start(f32[192]{0:T(256)} %get-tuple-element.149) | copy-start | bytes 2308
  175.8 11.7 %copy-start.74 = (f32[192]{0:T(256)S(1)}, f32[192]{0:T(256)}, u32[]{:S(2)}) copy-start(f32[192]{0:T(256)} %get-tuple-element.150) | copy-start | bytes 2308
  178.0 13.6 %copy-start.46 = (f32[4,192]{1,0:T(4,128)S(1)}, f32[4,192]{1,0:T(4,128)}, u32[]{:S(2)}) copy-start(f32[4,192]{1,0:T(4,128)} %add.435) | copy-start | bytes 9220
  178.0 13.6 %copy-start.47 = (f32[4,192]{1,0:T(4,128)S(1)}, f32[4,192]{1,0:T(4,128)}, u32[]{:S(2)}) copy-start(f32[4,192]{1,0:T(4,128)} %mul.370) | copy-start | bytes 9220
  181.7 18.4 %copy-start.68 = (s32[768]{0:T(1024)}, s32[768]{0:T(1024)S(1)}, u32[]{:S(2)}) copy-start(s32[768]{0:T(1024)S(1)} %reshape.897) | copy-start | bytes 9220
  303.6 11.4 %copy-start.13 = (f32[2,128,768]{2,1,0:T(8,128)S(1)}, f32[2,128,768]{2,1,0:T(8,128)}, u32[]{:S(2)}) copy-start(f32[2,128,768]{2,1,0:T(8,128)} %copy.314) | copy-start | bytes 2359300
  303.6 11.4 %copy-start.20 = (bf16[256,4,192]{0,2,1:T(8,128)(2,1)S(1)}, bf16[256,4,192]{0,2,1:T(8,128)(2,1)}, u32[]{:S(2)}) copy-start(bf16[256,4,192]{0,2,1:T(8,128)(2,1)} %copy.322) | copy-start | bytes 1179652
  303.6 11.4 %copy-start.40 = (f32[768]{0:T(1024)S(1)}, f32[768]{0:T(1024)}, u32[]{:S(2)}) copy-start(f32[768]{0:T(1024)} %add.445) | copy-start | bytes 9220
  340.4 19.9 %slice-start = ((s8[6291456]{0:T(1024)(128)(4,1)}), s8[2097152]{0:T(1024)(128)(4,1)S(1)}, s32[]{:S(2)}) async-start(s8[6291456]{0:T(1024)(128)(4,1)} %bitcast.518), calls=%async_computation.1 | async-start | bytes 4194304
  368.9 24.3 %copy-start.7 = (f32[2,128,768]{2,1,0:T(8,128)S(1)}, f32[2,128,768]{2,1,0:T(8,128)}, u32[]{:S(2)}) copy-start(f32[2,128,768]{2,1,0:T(8,128)} %copy.343) | copy-start | bytes 2359300
  370.2 25.1 %copy-start.64 = (f32[256]{0:T(256)S(1)}, f32[256]{0:T(256)}, u32[]{:S(2)}) copy-start(f32[256]{0:T(256)} %fusion.170) | copy-start | bytes 3076
  396.8 12.7 %copy-start.6 = (f32[2,4,1,48,512]{4,3,1,0,2:T(8,128)S(1)}, f32[2,4,1,48,512]{4,3,1,0,2:T(8,128)}, u32[]{:S(2)}) copy-start(f32[2,4,1,48,512]{4,3,1,0,2:T(8,128)} %copy-done.5) | copy-start | bytes 2359300
  396.8 12.7 %copy-start.55 = (f32[1,192]{1,0:T(1,128)S(1)}, f32[1,192]{1,0:T(1,128)}, u32[]{:S(2)}) copy-start(f32[1,192]{1,0:T(1,128)} %copy-done.54) | copy-start | bytes 2308
  412.2 9.9 %copy-start.3 = (bf16[4,8,48,768]{3,2,1,0:T(8,128)(2,1)S(1)}, bf16[4,8,48,768]{3,2,1,0:T(8,128)(2,1)}, u32[]{:S(2)}) copy-start(bf16[4,8,48,768]{3,2,1,0:T(8,128)(2,1)} %copy-done.2) | copy-start | bytes 7077892
  446.0 8.8 %copy-start.59 = (pred[2,512]{1,0:T(4,128)(4,1)S(1)}, pred[2,512]{1,0:T(4,128)(4,1)}, u32[]{:S(2)}) copy-start(pred[2,512]{1,0:T(4,128)(4,1)} %get-tuple-element.205) | copy-start | bytes 3076
  511.4 9.4 %copy-start.28 = (bf16[128,2,512]{2,1,0:T(2,128)(2,1)S(1)}, bf16[128,2,512]{2,1,0:T(2,128)(2,1)}, u32[]{:S(2)}) copy-start(bf16[128,2,512]{2,1,0:T(2,128)(2,1)} %copy.378) | copy-start | bytes 786436
  (64 other events, 214.9 us)
Sparse Core Ops, SparseCore 0:
  27.1 79.0 all-gather.2
